TPU v7x, 32 devices: a whole 2x2x4 slice. The times are simulated.
32 devices in a mesh: ctx: 8 (over z, x), tp: 4 (over y, core).
Axes of the slice: x: 2, y: 2, z: 4, core: 2. Of those that a mesh axis runs over, the one named last changes fastest.
Arguments:
- x_inputs: bfloat16 [4096, 4096], P('ctx', 'tp'), may hold values from -6 to 6
- state_maps: bfloat16 [4096, 1024], P('ctx', 'tp'), may hold values from -6 to 6
- z_gate: bfloat16 [4096, 4096], P('ctx', 'tp'), may hold values from -6 to 6
- step_raw: float32 [4096, 64], P('ctx', 'tp'), may hold values from -3 to 3
- step_bias: float32 [64], P('tp'), may hold values from -0.5 to 0.5
- decay_log: float32 [64], P('tp'), may hold values from -20 to -2
- skip_gain: float32 [64], P('tp'), may hold values from 0.5 to 1.5
- x_filter: bfloat16 [4, 4096], P(None, 'tp'), may hold values from -3 to 3
- state_filter: bfloat16 [4, 1024], P(None, 'tp'), may hold values from -3 to 3
- norm_gain: float32 [4096], P('tp'), may hold values from 0.1 to 1.9
- out_weight: bfloat16 [4096, 4096], P('tp'), may hold values from -0.09375 to 0.09375
Outputs:
- mixed: bfloat16 [4096, 4096], P(('ctx', 'tp'))
All inputs are finite; a program needn't handle non-finite values.
Results may differ from a plain program's by a relative error of at most 0.017.
Values may be sent and summed in bfloat16 or wider, within the bound.
A program may use at most 128 MiB of HBM per device.

v0:
```python
import jax
import jax.numpy as jnp
from jax import lax
from jax.sharding import PartitionSpec as P


def shifted(value, axis, steps):
    count = lax.axis_size(axis)
    leading, last = (max(0, -steps), min(count, count - steps))
    return lax.ppermute(value, axis, [(source, source + steps) for source in range(leading, last)])


def causal_conv(padded, filters, length):
    total = jnp.zeros((length, padded.shape[1]), jnp.float32)
    for offset in range(filters.shape[0]):
        total = total + filters[offset].astype(jnp.float32) * padded[
            offset : offset + length
        ].astype(jnp.float32)
    return total


def block_scan(values, b_rows, c_rows, log_decay, step_size, span):
    length, head_count, head_dim = values.shape
    state_size = b_rows.shape[1]
    pieces = length // span
    inputs = (
        values.reshape(pieces, span, head_count, head_dim),
        b_rows.reshape(pieces, span, state_size),
        c_rows.reshape(pieces, span, state_size),
        log_decay.reshape(pieces, span, head_count),
        step_size.reshape(pieces, span, head_count),
    )
    row_ids = lax.broadcasted_iota(jnp.int32, (span, span), 0)
    col_ids = lax.broadcasted_iota(jnp.int32, (span, span), 1)
    causal = (row_ids >= col_ids)[None]

    def advance(carried, piece):
        piece_x, piece_b, piece_c, piece_rate, piece_step = piece
        cumulative = jnp.cumsum(piece_rate, axis=0)
        by_head = cumulative.T
        spread = by_head[:, :, None] - by_head[:, None, :]
        decay = jnp.where(causal, jnp.exp(-jnp.where(causal, spread, 0.0)), 0.0)
        scores = jnp.dot(piece_c, piece_b.T, preferred_element_type=jnp.float32)
        weights = (decay * scores[None] * piece_step.T[:, None, :]).astype(jnp.bfloat16)
        output = jnp.einsum("hts,shp->thp", weights, piece_x, preferred_element_type=jnp.float32)
        rounded = carried.astype(jnp.bfloat16)
        output = (
            output
            + jnp.einsum("tn,hpn->thp", piece_c, rounded, preferred_element_type=jnp.float32)
            * jnp.exp(-cumulative)[:, :, None]
        )
        tail = jnp.exp(-(cumulative[-1][None, :] - cumulative)) * piece_step
        weighted = (tail[:, :, None] * piece_x.astype(jnp.float32)).astype(jnp.bfloat16)
        fresh = jnp.exp(-cumulative[-1])[:, None, None] * carried
        fresh = fresh + jnp.einsum(
            "shp,sn->hpn", weighted, piece_b, preferred_element_type=jnp.float32
        )
        return (fresh, output)

    start_state = jnp.zeros((head_count, head_dim, state_size), jnp.float32)
    final_state, outputs = lax.scan(advance, start_state, inputs)
    return (outputs.reshape(length, head_count, head_dim), final_state)


def on_device(
    x_inputs,
    state_maps,
    z_gate,
    step_raw,
    step_bias,
    decay_log,
    skip_gain,
    x_filter,
    state_filter,
    norm_gain,
    out_weight,
):
    length = x_inputs.shape[0]
    leading = x_filter.shape[0] - 1
    channels = x_inputs.shape[1]
    head_count = step_raw.shape[1]
    head_dim = channels // head_count
    state_size = state_maps.shape[1] // 2
    prev_x, prev_maps = shifted(
        (x_inputs[length - leading :], state_maps[length - leading :]), "ctx", 1
    )
    x_conv = jax.nn.silu(
        causal_conv(jnp.concatenate([prev_x, x_inputs], 0), x_filter, length)
    ).astype(jnp.bfloat16)
    bc_conv = jax.nn.silu(
        causal_conv(jnp.concatenate([prev_maps, state_maps], 0), state_filter, length)
    ).astype(jnp.bfloat16)
    step_size = jax.nn.softplus(step_raw + step_bias)
    log_decay = step_size * jnp.exp(decay_log)
    values = x_conv.reshape(length, head_count, head_dim)
    b_rows = bc_conv[:, :state_size]
    c_rows = bc_conv[:, state_size:]
    local_out, local_state = block_scan(
        values, b_rows, c_rows, log_decay, step_size, min(length, 512)
    )
    block_decay = jnp.exp(-jnp.sum(log_decay, axis=0))
    block_count = lax.axis_size("ctx")

    def relay_turn(index, carry_pair):
        incoming = shifted(carry_pair[1], "ctx", 1)
        return (incoming, block_decay[:, None, None] * incoming + local_state)

    carried, _ = lax.fori_loop(
        0, block_count - 1, relay_turn, (jnp.zeros_like(local_state), local_state)
    )
    cumulative = jnp.cumsum(log_decay, axis=0)
    rounded = carried.astype(jnp.bfloat16)
    output = (
        local_out
        + jnp.einsum("tn,hpn->thp", c_rows, rounded, preferred_element_type=jnp.float32)
        * jnp.exp(-cumulative)[:, :, None]
    )
    output = output + skip_gain[None, :, None] * values.astype(jnp.float32)
    gated = output.reshape(length, channels) * jax.nn.silu(z_gate.astype(jnp.float32))
    scale = lax.rsqrt(jnp.mean(gated * gated, axis=-1, keepdims=True) + 1e-05)
    normed = (gated * scale * norm_gain).astype(jnp.bfloat16)
    return lax.psum_scatter(
        jnp.dot(normed, out_weight, preferred_element_type=jnp.float32).astype(jnp.bfloat16),
        "tp",
        scatter_dimension=0,
        tiled=True,
    )


def solution(mesh):
    return jax.shard_map(
        on_device,
        mesh=mesh,
        in_specs=(
            P("ctx", "tp"),
            P("ctx", "tp"),
            P("ctx", "tp"),
            P("ctx", "tp"),
            P("tp"),
            P("tp"),
            P("tp"),
            P(None, "tp"),
            P(None, "tp"),
            P("tp"),
            P("tp", None),
        ),
        out_specs=P(("ctx", "tp"), None),
        check_vma=False,
    )
```

profile of v0, /device:TPU:25, one launch (start us, length us, event | category | flops | bytes accessed | tf_op | source)
XLA Modules:
  0.0 210.5 jit_solution(8407593463671130301)
XLA Ops:
  7.2 3.1 %collective-permute-start.2 = (bf16[3,256]{1,0:T(4,128)(2,1)S(1)}, bf16[3,256]{1,0:T(4,128)(2,1)S(1)}, u32[]{:S(2)}, u32[]{:S(2)}) collective-permute-start(bf16[3,256]{1,0:T(4,128)(2,1)S(1)} %slice.78), channel_id=1, source_target_pairs={{0,4},{4,8},{8,12},{12,16},{16,20},{20,24},{24,28},{1,5},{5,9},{9,... | collective-permute-start | bytes 4616 | tf_op jit(solution)/shard_map/ppermute | solution.py:10
  11.1 1.9 collective-permute-start.1
  20.7 1.9 multiply_convert_fusion.7
  24.9 3.9 %multiply_convert_fusion.3 = bf16[512,1024]{1,0:T(8,128)(2,1)S(1)} fusion(bf16[512,1024]{1,0:T(8,128)(2,1)} %param.13, bf16[3,1024]{1,0:T(4,128)(2,1)} %copy-done.6, f32[1024]{0:T(1024)S(1)} %bitcast.56, f32[1024]{0:T(1024)S(1)} %bitcast.57, f32[1024]{0:T(1024)S(1)} %bitcast.55, f32[1024]{0:T(1024)S(1)} %bitcast.54), kind=kLoop, calls=%fused_computation.19 | loop fusion | flops 13107200 | bytes 2119680 | tf_op jit(solution)/shard_map/convert_element_type | solution.py:89
  30.2 1.7 convolution_add_fusion
  32.7 97.4 %while.2 = (s32[]{:T(128)}, f32[16,64,128]{2,1,0:T(8,128)}, f32[16,64,128]{2,1,0:T(8,128)}, f32[16]{0:T(128)S(1)}, f32[16,64,128]{2,1,0:T(8,128)S(1)}, /*index=5*/s32[]{:T(128)}) while((s32[]{:T(128)}, f32[16,64,128]{2,1,0:T(8,128)}, f32[16,64,128]{2,1,0:T(8,128)}, f32[16]{0:T(128)S(1)}, f32[16,64,128]{2,1,0:T(8,128)S(1)}, ...), condition=%wide.region_4.5_spmd, body=%wide.region_3.4_spmd.sunk | while | flops 262146 | bytes 5767369 | solution.py:108
  32.7 1.9 collective-permute-start
  34.6 13.5 %collective-permute-done = f32[16,64,128]{2,1,0:T(8,128)S(1)} collective-permute-done((f32[16,64,128]{2,1,0:T(8,128)}, f32[16,64,128]{2,1,0:T(8,128)S(1)}, u32[]{:S(2)}, u32[]{:S(2)}) %collective-permute-start) | collective-permute-done | bytes 524320 | tf_op jit(solution)/shard_map/while/body/eval_jaxpr/ppermute | solution.py:10
  49.1 1.9 collective-permute-start
  51.1 12.6 %collective-permute-done = f32[16,64,128]{2,1,0:T(8,128)S(1)} collective-permute-done((f32[16,64,128]{2,1,0:T(8,128)}, f32[16,64,128]{2,1,0:T(8,128)S(1)}, u32[]{:S(2)}, u32[]{:S(2)}) %collective-permute-start) | collective-permute-done | bytes 524320 | tf_op jit(solution)/shard_map/while/body/eval_jaxpr/ppermute | solution.py:10
  64.7 1.9 collective-permute-start
  66.6 11.7 %collective-permute-done = f32[16,64,128]{2,1,0:T(8,128)S(1)} collective-permute-done((f32[16,64,128]{2,1,0:T(8,128)}, f32[16,64,128]{2,1,0:T(8,128)S(1)}, u32[]{:S(2)}, u32[]{:S(2)}) %collective-permute-start) | collective-permute-done | bytes 524320 | tf_op jit(solution)/shard_map/while/body/eval_jaxpr/ppermute | solution.py:10
  79.4 1.9 collective-permute-start
  81.3 10.8 %collective-permute-done = f32[16,64,128]{2,1,0:T(8,128)S(1)} collective-permute-done((f32[16,64,128]{2,1,0:T(8,128)}, f32[16,64,128]{2,1,0:T(8,128)S(1)}, u32[]{:S(2)}, u32[]{:S(2)}) %collective-permute-start) | collective-permute-done | bytes 524320 | tf_op jit(solution)/shard_map/while/body/eval_jaxpr/ppermute | solution.py:10
  93.1 1.9 collective-permute-start
  95.0 9.9 %collective-permute-done = f32[16,64,128]{2,1,0:T(8,128)S(1)} collective-permute-done((f32[16,64,128]{2,1,0:T(8,128)}, f32[16,64,128]{2,1,0:T(8,128)S(1)}, u32[]{:S(2)}, u32[]{:S(2)}) %collective-permute-start) | collective-permute-done | bytes 524320 | tf_op jit(solution)/shard_map/while/body/eval_jaxpr/ppermute | solution.py:10
  105.9 1.9 collective-permute-start
  107.8 9.1 %collective-permute-done = f32[16,64,128]{2,1,0:T(8,128)S(1)} collective-permute-done((f32[16,64,128]{2,1,0:T(8,128)}, f32[16,64,128]{2,1,0:T(8,128)S(1)}, u32[]{:S(2)}, u32[]{:S(2)}) %collective-permute-start) | collective-permute-done | bytes 524320 | tf_op jit(solution)/shard_map/while/body/eval_jaxpr/ppermute | solution.py:10
  118.0 1.9 collective-permute-start
  119.9 9.1 %collective-permute-done = f32[16,64,128]{2,1,0:T(8,128)S(1)} collective-permute-done((f32[16,64,128]{2,1,0:T(8,128)}, f32[16,64,128]{2,1,0:T(8,128)S(1)}, u32[]{:S(2)}, u32[]{:S(2)}) %collective-permute-start) | collective-permute-done | bytes 524320 | tf_op jit(solution)/shard_map/while/body/eval_jaxpr/ppermute | solution.py:10
  131.7 7.2 %fusion.3 = f32[512,16,64]{0,2,1:T(8,128)} fusion(bf16[512,16,64]{0,2,1:T(8,128)(2,1)S(1)} %bitcast.52, f32[512,16,64]{0,2,1:T(8,128)S(1)} %fusion.17, f32[512,16,64]{0,2,1:T(8,128)S(1)} %fusion.21, f32[16,512]{1,0:T(8,128)S(1)} %get-tuple-element.71, f32[512,512]{1,0:T(8,128)S(1)} %copy-done.1, f32[16,512]{1,0:T(8,128)S(1)} %get-tuple-element.74, ...), kind=kOutput, calls=%fused_computation.10 | convolution fusion | flops 569901056 | bytes 8749120 | tf_op jit(solution)/shard_map/while/body/eval_jaxpr/hts,shp->thp/dot_general | solution.py:45
  138.9 2.0 copy.18
  141.7 10.0 %convolution_convert_fusion = bf16[512,4096]{1,0:T(8,128)(2,1)} fusion(bf16[1024,4096]{1,0:T(8,128)(2,1)} %param.23, f32[1024]{0:T(1024)S(1)} %copy-done.7, f32[512]{0:T(512)S(1)} %add_rsqrt_fusion, f32[512,1024]{1,0:T(8,128)S(1)} %copy.18, bf16[512,1024]{1,0:T(8,128)(2,1)S(1)} %copy-done.3), kind=kOutput, calls=%fused_computation.4 | convolution fusion | flops 4301783040 | bytes 15734784 | tf_op jit(solution)/shard_map/dot_general | solution.py:123
  151.7 51.9 %reduce-scatter.2.cloned.1.call-done = bf16[128,4096]{1,0:T(8,128)(2,1)} async-done(((bf16[512,4096]{1,0:T(8,128)(2,1)}), bf16[128,4096]{1,0:T(8,128)(2,1)}) %reduce-scatter.2.cloned.1.call-update) | async-done | bytes 1048592 | tf_op jit(solution)/shard_map/reduce_scatter | solution.py:122
  (68 shorter events, 23.2 us)
Async XLA Ops:
  6.5 197.1 %reduce-scatter.2.cloned.1.call-start = ((), (), s32[]{:S(2)}) async-start(), calls=%async_computation.1 | async-start | bytes 5242880 | tf_op jit(solution)/shard_map/reduce_scatter | solution.py:122
  7.2 13.5 %collective-permute-start.2 = (bf16[3,256]{1,0:T(4,128)(2,1)S(1)}, bf16[3,256]{1,0:T(4,128)(2,1)S(1)}, u32[]{:S(2)}, u32[]{:S(2)}) collective-permute-start(bf16[3,256]{1,0:T(4,128)(2,1)S(1)} %slice.78), channel_id=1, source_target_pairs={{0,4},{4,8},{8,12},{12,16},{16,20},{20,24},{24,28},{1,5},{5,9},{9,... | collective-permute-start | bytes 4616 | tf_op jit(solution)/shard_map/ppermute | solution.py:10
  11.1 13.3 %collective-permute-start.1 = (bf16[3,1024]{1,0:T(4,128)(2,1)S(1)}, bf16[3,1024]{1,0:T(4,128)(2,1)S(1)}, u32[]{:S(2)}, u32[]{:S(2)}) collective-permute-start(bf16[3,1024]{1,0:T(4,128)(2,1)S(1)} %slice.68), channel_id=1, source_target_pairs={{0,4},{4,8},{8,12},{12,16},{16,20},{20,24},{24,28},{1,5},{5,9},{9,... | collective-permute-start | bytes 18440 | tf_op jit(solution)/shard_map/ppermute | solution.py:10
  28.8 1.3 copy-start.9
  28.8 3.8 %copy-start.5 = (f32[16]{0:T(128)S(1)}, f32[16]{0:T(128)}, u32[]{:S(2)}) copy-start(f32[16]{0:T(128)} %negate_exponential_fusion.1) | copy-start | bytes 196
  32.7 15.5 %collective-permute-start = (f32[16,64,128]{2,1,0:T(8,128)}, f32[16,64,128]{2,1,0:T(8,128)S(1)}, u32[]{:S(2)}, u32[]{:S(2)}) collective-permute-start(f32[16,64,128]{2,1,0:T(8,128)} %get-tuple-element.121), channel_id=1, source_target_pairs={{0,4},{4,8},{8,12},{12,16},{16,20},{20,24},{24,28},{1,5},{5,9},{9,... | collective-permute-start | bytes 1572872 | tf_op jit(solution)/shard_map/while/body/eval_jaxpr/ppermute | solution.py:10
  48.1 1.0 copy-start
  49.1 14.5 %collective-permute-start = (f32[16,64,128]{2,1,0:T(8,128)}, f32[16,64,128]{2,1,0:T(8,128)S(1)}, u32[]{:S(2)}, u32[]{:S(2)}) collective-permute-start(f32[16,64,128]{2,1,0:T(8,128)} %get-tuple-element.121), channel_id=1, source_target_pairs={{0,4},{4,8},{8,12},{12,16},{16,20},{20,24},{24,28},{1,5},{5,9},{9,... | collective-permute-start | bytes 1572872 | tf_op jit(solution)/shard_map/while/body/eval_jaxpr/ppermute | solution.py:10
  63.7 1.0 copy-start
  64.7 13.6 %collective-permute-start = (f32[16,64,128]{2,1,0:T(8,128)}, f32[16,64,128]{2,1,0:T(8,128)S(1)}, u32[]{:S(2)}, u32[]{:S(2)}) collective-permute-start(f32[16,64,128]{2,1,0:T(8,128)} %get-tuple-element.121), channel_id=1, source_target_pairs={{0,4},{4,8},{8,12},{12,16},{16,20},{20,24},{24,28},{1,5},{5,9},{9,... | collective-permute-start | bytes 1572872 | tf_op jit(solution)/shard_map/while/body/eval_jaxpr/ppermute | solution.py:10
  78.3 1.0 copy-start
  79.4 12.7 %collective-permute-start = (f32[16,64,128]{2,1,0:T(8,128)}, f32[16,64,128]{2,1,0:T(8,128)S(1)}, u32[]{:S(2)}, u32[]{:S(2)}) collective-permute-start(f32[16,64,128]{2,1,0:T(8,128)} %get-tuple-element.121), channel_id=1, source_target_pairs={{0,4},{4,8},{8,12},{12,16},{16,20},{20,24},{24,28},{1,5},{5,9},{9,... | collective-permute-start | bytes 1572872 | tf_op jit(solution)/shard_map/while/body/eval_jaxpr/ppermute | solution.py:10
  92.1 1.0 copy-start
  93.1 11.8 %collective-permute-start = (f32[16,64,128]{2,1,0:T(8,128)}, f32[16,64,128]{2,1,0:T(8,128)S(1)}, u32[]{:S(2)}, u32[]{:S(2)}) collective-permute-start(f32[16,64,128]{2,1,0:T(8,128)} %get-tuple-element.121), channel_id=1, source_target_pairs={{0,4},{4,8},{8,12},{12,16},{16,20},{20,24},{24,28},{1,5},{5,9},{9,... | collective-permute-start | bytes 1572872 | tf_op jit(solution)/shard_map/while/body/eval_jaxpr/ppermute | solution.py:10
  104.9 1.0 copy-start
  105.9 11.0 %collective-permute-start = (f32[16,64,128]{2,1,0:T(8,128)}, f32[16,64,128]{2,1,0:T(8,128)S(1)}, u32[]{:S(2)}, u32[]{:S(2)}) collective-permute-start(f32[16,64,128]{2,1,0:T(8,128)} %get-tuple-element.121), channel_id=1, source_target_pairs={{0,4},{4,8},{8,12},{12,16},{16,20},{20,24},{24,28},{1,5},{5,9},{9,... | collective-permute-start | bytes 1572872 | tf_op jit(solution)/shard_map/while/body/eval_jaxpr/ppermute | solution.py:10
  116.9 1.0 copy-start
  118.0 11.0 %collective-permute-start = (f32[16,64,128]{2,1,0:T(8,128)}, f32[16,64,128]{2,1,0:T(8,128)S(1)}, u32[]{:S(2)}, u32[]{:S(2)}) collective-permute-start(f32[16,64,128]{2,1,0:T(8,128)} %get-tuple-element.121), channel_id=1, source_target_pairs={{0,4},{4,8},{8,12},{12,16},{16,20},{20,24},{24,28},{1,5},{5,9},{9,... | collective-permute-start | bytes 1572872 | tf_op jit(solution)/shard_map/while/body/eval_jaxpr/ppermute | solution.py:10
  129.0 1.0 copy-start
  130.0 1.6 copy-start.1
  130.0 1.7 copy-start.2
  130.0 1.7 copy-start.4
  130.0 1.7 copy-start.8
  138.9 2.0 copy-start.3
  (2 other events, 1.3 us)
Sparse Core Ops, SparseCore 0:
  151.8 51.7 reduce-scatter.1
where the time goes:
time: 213 us; the launch traced here: 210 us
  waiting for transfers between devices  129 us (61%)
  matrix products  22.2 us (10%)
  other arithmetic  20.3 us (10%)
  starting transfers between devices  18.4 us (9%)
  between operations  13.5 us (6%)
  local copies, waits for them, and re-layouts  7.31 us (3%)
    ppermute x9, waiting for transfers between devices, shifted(): lax.ppermute(value, axis, [(source, source + steps) for source in range(l...  76.7 us
    reduce_scatter x1, waiting for transfers between devices, on_device(): lax.psum_scatter(jnp.dot(normed, out_weight, preferred_element_type=jnp.f...  51.9 us
    ppermute x9, starting transfers between devices, shifted(): lax.ppermute(value, axis, [(source, source + steps) for source in range(l...  18.4 us
    dot_general x1, matrix products, on_device(): jnp.dot(normed, out_weight, preferred_element_type=jnp.float32)  10 us
    dot_general x1, matrix products, advance(): jnp.einsum('hts,shp->thp', weights, piece_x, preferred_element_type=jnp.f...  7.16 us
    add x7, other arithmetic, relay_turn(): return (incoming, block_decay[:, None, None] * incoming + local_state)  7.16 us
  transfers between devices with their start and end apart: 10, of which 8 were waited for; matrix products, arithmetic and copies ran while one was open for 6% of the time, Pallas kernels for 0%

commit v1 on v0

v1 whole, which is shorter than its diff:
```python
import functools

import jax
import jax.numpy as jnp
from jax import lax
from jax.experimental import pallas as pl
from jax.experimental.pallas import tpu as pltpu
from jax.sharding import PartitionSpec as P

MESH = pl.DeviceIdType.MESH
LANES = 128
HALO = 16


def half_silu(v):
    h = 0.5 * v
    return h + h * jnp.tanh(h)


def layer_kernel(
    n_ctx, n_tp, chunk,
    x_ref, m_ref, z_ref, step_ref, bias_ref, decay_ref, skip_ref, xf_ref, mf_ref, gain_ref, w_hbm,
    out_ref,
    w_ref, hx_ref, hm_ref, pad_ref, xfs_ref, mfs_ref, gains_ref, skips_ref,
    col_ref, sq_ref, at_ref, rt_ref, aexp_ref, dsend_ref, drecv_ref,
    xc_ref, bt_ref, c_ref, cb_ref, lown_ref, lsend_ref, lrecv_ref, csend_ref, crecv_ref, sr_ref,
    yg_ref, eg_ref, gated_ref, normed_ref, part_ref, core_ref, ysend_ref, yrecv_ref,
    w_sem, halo_send, halo_recv, dec_send, dec_recv, pair_send, pair_recv, chain_send, chain_recv,
    core_send, core_recv, y_send, y_recv,
):
    length = x_ref.shape[0]
    pairs = x_ref.shape[1] // LANES
    heads = step_ref.shape[1]
    n_y = n_tp // 2
    rows = length // n_tp
    n_chunks = w_hbm.shape[1] // chunk
    n_z = n_ctx // 2
    ctx = lax.axis_index("ctx")
    tp = lax.axis_index("tp")
    y, core = tp // 2, tp % 2
    z, odd = ctx // 2, ctx % 2
    mate = ctx + 1 - 2 * odd
    other_core = y * 2 + 1 - core

    w_copy = pltpu.make_async_copy(w_hbm, w_ref, w_sem)
    w_copy.start()

    barrier = pltpu.get_barrier_semaphore()
    for off in (1, n_ctx - 1, 2, n_ctx - 2):
        pl.semaphore_signal(barrier, inc=1, device_id={"ctx": (ctx + off) % n_ctx}, device_id_type=MESH)
    pl.semaphore_signal(barrier, inc=1, device_id={"tp": other_core}, device_id_type=MESH)
    for off in range(1, n_y):
        pl.semaphore_signal(
            barrier, inc=1, device_id={"tp": ((y + off) % n_y) * 2 + core}, device_id_type=MESH
        )
    pl.semaphore_wait(barrier, 4 + 1 + (n_y - 1))

    def remote(src, dst, send, recv, where):
        return pltpu.make_async_remote_copy(
            src_ref=src, dst_ref=dst, send_sem=send, recv_sem=recv, device_id=where, device_id_type=MESH
        )

    following = {"ctx": (ctx + 1) % n_ctx}
    halo_x = remote(x_ref.at[pl.ds(length - HALO, HALO)], hx_ref, halo_send.at[0], halo_recv.at[0], following)
    halo_m = remote(m_ref.at[pl.ds(length - HALO, HALO)], hm_ref, halo_send.at[1], halo_recv.at[1], following)
    halo_m.start()
    halo_x.start()

    step = jnp.log(1.0 + jnp.exp(step_ref[...] + bias_ref[...]))
    col_ref[...] = jnp.zeros_like(col_ref)
    col_ref[:, :heads] = step * jnp.exp(decay_ref[...])
    rate_t = col_ref[...].T[:heads]
    col_ref[:, :heads] = jnp.log(step)
    log_step_t = col_ref[...].T[:heads]
    s_ids = lax.broadcasted_iota(jnp.int32, (length, length), 0)
    t_ids = lax.broadcasted_iota(jnp.int32, (length, length), 1)
    upper = jnp.where(s_ids <= t_ids, 1.0, 0.0).astype(jnp.float32)
    sums = jnp.dot(rate_t, upper, precision=lax.Precision.HIGHEST, preferred_element_type=jnp.float32)
    at_ref[...] = sums
    rt_ref[...] = sums + log_step_t
    sq_ref[...] = jnp.zeros_like(sq_ref)
    sq_ref[:, :heads] = jnp.broadcast_to(skip_ref[...], (LANES, heads))
    skip_t = sq_ref[...].T
    lane_row = lax.broadcasted_iota(jnp.int32, (1, LANES), 1) < LANES // 2
    x_taps = xf_ref[...].astype(jnp.float32)
    m_taps = mf_ref[...].astype(jnp.float32)
    for p in range(pairs):
        skips_ref[p] = jnp.broadcast_to(
            jnp.where(lane_row, skip_t[2 * p : 2 * p + 1], skip_t[2 * p + 1 : 2 * p + 2]), (8, LANES)
        )
        gains_ref[p] = jnp.broadcast_to(gain_ref[:, p * LANES : (p + 1) * LANES], (8, LANES))
        xfs_ref[p] = x_taps[:, p * LANES : (p + 1) * LANES]
    for p in range(2):
        mfs_ref[p] = m_taps[:, p * LANES : (p + 1) * LANES]

    head_sub = lax.broadcasted_iota(jnp.int32, (LANES, length), 0) < LANES // 2

    def by_pair(ref, p):
        return jnp.where(head_sub, ref[pl.ds(2 * p, 1), :], ref[pl.ds(2 * p + 1, 1), :]).T

    def expand(p, _):
        spread = by_pair(at_ref, p)
        aexp_ref[p] = spread
        dsend_ref[p] = jnp.broadcast_to(spread[length - 1 : length], (8, LANES))
        return 0

    lax.fori_loop(0, pairs, expand, 0)
    dec_copy = remote(dsend_ref, drecv_ref, dec_send, dec_recv, {"ctx": mate})
    dec_copy.start()

    taps = xf_ref.shape[0]
    has_prev = jnp.where(ctx > 0, 1.0, 0.0).astype(jnp.float32)

    def conv(block, halo, filters):
        pad_ref[0:8] = halo.astype(jnp.float32)[HALO - 8 :] * has_prev
        pad_ref[8:] = block.astype(jnp.float32)
        total = filters[0:1] * pad_ref[9 - taps : 9 - taps + length]
        for k in range(1, taps):
            start = 9 - taps + k
            total = total + filters[k : k + 1] * pad_ref[start : start + length]
        return half_silu(total)

    halo_m.wait_recv()
    bt_ref[...] = conv(m_ref[:, :LANES], hm_ref[:, :LANES], mfs_ref[0]).T.astype(jnp.bfloat16)
    c_ref[...] = conv(m_ref[:, LANES:], hm_ref[:, LANES:], mfs_ref[1]).astype(jnp.bfloat16)
    halo_x.wait_recv()

    def pair_copy(p):
        return remote(lsend_ref.at[p], lrecv_ref.at[p], pair_send.at[p], pair_recv.at[p], {"ctx": mate})

    def local_state(p, _):
        cols = pl.ds(pl.multiple_of(p * LANES, LANES), LANES)
        xc = conv(x_ref[:, cols], hx_ref[:, cols], xfs_ref[p]).astype(jnp.bfloat16)
        xc_ref[p] = xc
        tail = jnp.exp(by_pair(rt_ref, p) - dsend_ref[p][0:1])
        u = (tail * xc.astype(jnp.float32)).astype(jnp.bfloat16)
        state = jnp.dot(bt_ref[...], u, preferred_element_type=jnp.float32)
        lown_ref[p] = state
        lsend_ref[p] = state.astype(jnp.bfloat16)
        pair_copy(p).start()
        return 0

    lax.fori_loop(0, pairs, local_state, 0)

    scores = jnp.dot(c_ref[...], bt_ref[...], preferred_element_type=jnp.float32)
    cb_ref[...] = jnp.where(s_ids >= t_ids, scores, 0.0)

    is_odd = odd.astype(jnp.float32)
    is_even = 1.0 - is_odd
    next_pair = {"ctx": (ctx + 2) % n_ctx}

    def chain_copy(p):
        return remote(csend_ref.at[p], crecv_ref.at[p], chain_send.at[p], chain_recv.at[p], next_pair)

    @pl.when(z == 0)
    def _():
        crecv_ref[...] = jnp.zeros_like(crecv_ref)

    dec_copy.wait_recv()

    def relay(p):
        pair_copy(p).wait_recv()
        mine = lown_ref[p]
        theirs = lrecv_ref[p].astype(jnp.float32)
        d_mine = jnp.exp(-dsend_ref[p][0:1])
        d_theirs = jnp.exp(-drecv_ref[p][0:1])
        l_even = mine * is_even + theirs * is_odd
        l_odd = mine * is_odd + theirs * is_even
        d_even = d_mine * is_even + d_theirs * is_odd
        d_odd = d_mine * is_odd + d_theirs * is_even

        @pl.when(z > 0)
        def _():
            chain_copy(p).wait_recv()

        entering = crecv_ref[p].astype(jnp.float32)
        middle = d_even * entering + l_even
        sr_ref[p] = (entering * is_even + middle * is_odd).astype(jnp.bfloat16)

        @pl.when(z < n_z - 1)
        def _():
            csend_ref[p] = (d_odd * middle + l_odd).astype(jnp.bfloat16)
            chain_copy(p).start()

    half = length // 2
    low_lanes = lax.broadcasted_iota(jnp.int32, (half, LANES), 1) < LANES // 2

    def within(p):
        xc = xc_ref[p]
        tops, bottoms = [], []
        for h in range(2):
            row_r = rt_ref[pl.ds(2 * p + h, 1), :]
            col_a = jnp.broadcast_to(at_ref[pl.ds(2 * p + h, 1), :], (LANES, length)).T
            col_a = jnp.concatenate([col_a] * (half // LANES), axis=1)

            def weigh(t0, s0, masked):
                power = row_r[:, s0 : s0 + half] - col_a[t0 : t0 + half]
                if masked:
                    power = jnp.minimum(power, 64.0)
                return (jnp.exp(power) * cb_ref[t0 : t0 + half, s0 : s0 + half]).astype(jnp.bfloat16)

            tops.append(jnp.dot(weigh(0, 0, True), xc[:half], preferred_element_type=jnp.float32))
            bottoms.append(
                jnp.dot(weigh(half, 0, False), xc[:half], preferred_element_type=jnp.float32)
                + jnp.dot(weigh(half, half, True), xc[half:], preferred_element_type=jnp.float32)
            )
        cols = pl.ds(pl.multiple_of(p * LANES, LANES), LANES)
        skip = skips_ref[p][0:1]
        for t0, both in ((0, tops), (half, bottoms)):
            here = pl.ds(t0, half)
            gate = half_silu(z_ref[here, cols].astype(jnp.float32))
            own = jnp.where(low_lanes, both[0], both[1])
            yg_ref[p, here] = (own + skip * xc[t0 : t0 + half].astype(jnp.float32)) * gate
            eg_ref[p, here] = jnp.exp(-aexp_ref[p, here]) * gate

    lag = jnp.minimum(2 * z, pairs)

    def turn(i, _):
        @pl.when((i >= lag) & (i < lag + pairs))
        def _():
            relay(i - lag)

        @pl.when(i < pairs)
        def _():
            within(i)

        return 0

    lax.fori_loop(0, 2 * pairs, turn, 0)

    span = 2 * rows
    channels = x_ref.shape[1]

    def project_rows(first):
        here = pl.ds(pl.multiple_of(first, span), span)
        c_rows = c_ref[here, :]

        def gate_pair(p, total):
            inter = jnp.dot(c_rows, sr_ref[p], preferred_element_type=jnp.float32)
            gated = yg_ref[p, here] + eg_ref[p, here] * inter
            gated_ref[p] = gated
            return total + gated * gated

        squares = lax.fori_loop(0, pairs, gate_pair, jnp.zeros((span, LANES), jnp.float32))
        scale = lax.rsqrt(jnp.sum(squares, axis=1, keepdims=True) / channels + 1e-05)
        for p in range(pairs):
            normed_ref[:, p * LANES : (p + 1) * LANES] = (
                gated_ref[p] * scale * gains_ref[p][0:1]
            ).astype(jnp.bfloat16)

    def core_copy(slot, k):
        return remote(
            part_ref.at[slot, k, 1 - core], core_ref.at[slot, k],
            core_send.at[slot, k], core_recv.at[slot, k], {"tp": other_core},
        )

    def y_copy(slot, k):
        target = ((y + slot) % n_y) * 2 + core
        return remote(
            ysend_ref.at[slot - 1, k], yrecv_ref.at[slot - 1, k],
            y_send.at[slot - 1, k], y_recv.at[slot - 1, k], {"tp": target},
        )

    def project(slot, k):
        cols = pl.ds(pl.multiple_of(k * chunk, chunk), chunk)
        part = jnp.dot(normed_ref[...], w_ref[:, cols], preferred_element_type=jnp.float32)
        part = part.astype(jnp.bfloat16)
        part_ref[slot, k, 0] = part[:rows]
        part_ref[slot, k, 1] = part[rows:]
        core_copy(slot, k).start()

    def chip_sum(slot, k):
        core_copy(slot, k).wait_recv()
        return part_ref[slot, k, core].astype(jnp.float32) + core_ref[slot, k].astype(jnp.float32)

    for slot in list(range(1, n_y)) + [0]:
        project_rows(((y + slot) % n_y) * span)
        if slot == (1 if n_y > 1 else 0):
            w_copy.wait()

        def forward(k, slot=slot):
            ysend_ref[slot - 1, k] = chip_sum(slot, k).astype(jnp.bfloat16)
            y_copy(slot, k).start()

        def column(k, _, slot=slot):
            project(slot, k)
            if slot > 0:

                @pl.when(k > 0)
                def _():
                    forward(k - 1)

            return 0

        lax.fori_loop(0, n_chunks, column, 0)
        if slot > 0:
            forward(n_chunks - 1)

    def finish(k, _):
        total = chip_sum(0, k)
        for slot in range(1, n_y):
            y_copy(slot, k).wait_recv()
            total = total + yrecv_ref[slot - 1, k].astype(jnp.float32)
        cols = pl.ds(pl.multiple_of(k * chunk, chunk), chunk)
        out_ref[:, cols] = total.astype(jnp.bfloat16)
        return 0

    lax.fori_loop(0, n_chunks, finish, 0)

    halo_m.wait_send()
    halo_x.wait_send()
    dec_copy.wait_send()

    def drain_states(p, _):
        pair_copy(p).wait_send()

        @pl.when(z < n_z - 1)
        def _():
            chain_copy(p).wait_send()

        return 0

    lax.fori_loop(0, pairs, drain_states, 0)

    def drain_parts(k, _):
        for slot in range(n_y):
            core_copy(slot, k).wait_send()
        for slot in range(1, n_y):
            y_copy(slot, k).wait_send()
        return 0

    lax.fori_loop(0, n_chunks, drain_parts, 0)


def on_device(n_ctx, n_tp, *args):
    (x_inputs, state_maps, z_gate, step_raw, step_bias, decay_log, skip_gain,
     x_filter, state_filter, norm_gain, out_weight) = args
    length, channels = x_inputs.shape
    heads = step_raw.shape[1]
    pairs = channels // LANES
    model = out_weight.shape[1]
    rows = length // n_tp
    n_y = n_tp // 2
    chunk = 512
    n_chunks = model // chunk
    state = state_maps.shape[1] // 2
    bf16, f32 = jnp.bfloat16, jnp.float32
    vmem = pl.BlockSpec(memory_space=pltpu.VMEM)
    dma = pltpu.SemaphoreType.DMA
    scratch = [
        pltpu.VMEM(out_weight.shape, bf16),
        pltpu.VMEM((HALO, channels), bf16),
        pltpu.VMEM((HALO, 2 * state), bf16),
        pltpu.VMEM((length + 8, LANES), f32),
        pltpu.VMEM((pairs, x_filter.shape[0], LANES), f32),
        pltpu.VMEM((2, x_filter.shape[0], LANES), f32),
        pltpu.VMEM((pairs, 8, LANES), f32),
        pltpu.VMEM((pairs, 8, LANES), f32),
        pltpu.VMEM((length, LANES), f32),
        pltpu.VMEM((LANES, LANES), f32),
        pltpu.VMEM((heads, length), f32),
        pltpu.VMEM((heads, length), f32),
        pltpu.VMEM((pairs, length, LANES), f32),
        pltpu.VMEM((pairs, 8, LANES), f32),
        pltpu.VMEM((pairs, 8, LANES), f32),
        pltpu.VMEM((pairs, length, LANES), bf16),
        pltpu.VMEM((state, length), bf16),
        pltpu.VMEM((length, state), bf16),
        pltpu.VMEM((length, length), f32),
        pltpu.VMEM((pairs, state, LANES), f32),
        pltpu.VMEM((pairs, state, LANES), bf16),
        pltpu.VMEM((pairs, state, LANES), bf16),
        pltpu.VMEM((pairs, state, LANES), bf16),
        pltpu.VMEM((pairs, state, LANES), bf16),
        pltpu.VMEM((pairs, state, LANES), bf16),
        pltpu.VMEM((pairs, length, LANES), f32),
        pltpu.VMEM((pairs, length, LANES), f32),
        pltpu.VMEM((pairs, 2 * rows, LANES), f32),
        pltpu.VMEM((2 * rows, channels), bf16),
        pltpu.VMEM((n_y, n_chunks, 2, rows, chunk), bf16),
        pltpu.VMEM((n_y, n_chunks, rows, chunk), bf16),
        pltpu.VMEM((n_y - 1, n_chunks, rows, chunk), bf16),
        pltpu.VMEM((n_y - 1, n_chunks, rows, chunk), bf16),
        dma, dma((2,)), dma((2,)), dma, dma,
        dma((pairs,)), dma((pairs,)), dma((pairs,)), dma((pairs,)),
        dma((n_y, n_chunks)), dma((n_y, n_chunks)),
        dma((n_y - 1, n_chunks)), dma((n_y - 1, n_chunks)),
    ]
    return pl.pallas_call(
        functools.partial(layer_kernel, n_ctx, n_tp, chunk),
        out_shape=jax.ShapeDtypeStruct((rows, model), bf16),
        in_specs=[vmem] * 10 + [pl.BlockSpec(memory_space=pl.ANY)],
        out_specs=vmem,
        scratch_shapes=scratch,
        compiler_params=pltpu.CompilerParams(
            collective_id=0, has_side_effects=True, vmem_limit_bytes=58 * 1024 * 1024
        ),
        cost_estimate=pl.CostEstimate(
            flops=2 * length * channels * (model + 2 * length), bytes_accessed=4 * out_weight.size,
            transcendentals=length * length * heads,
        ),
        name="layer",
    )(
        x_inputs, state_maps, z_gate, step_raw, step_bias[None], decay_log[None], skip_gain[None],
        x_filter, state_filter, norm_gain[None], out_weight,
    )


def solution(mesh):
    return jax.shard_map(
        functools.partial(on_device, mesh.shape["ctx"], mesh.shape["tp"]),
        mesh=mesh,
        in_specs=(
            P("ctx", "tp"),
            P("ctx", "tp"),
            P("ctx", "tp"),
            P("ctx", "tp"),
            P("tp"),
            P("tp"),
            P("tp"),
            P(None, "tp"),
            P(None, "tp"),
            P("tp"),
            P("tp", None),
        ),
        out_specs=P(("ctx", "tp"), None),
        check_vma=False,
    )
```

time: 213 us -> 58.6 us (0.28); the launches traced: 210 us -> 58.3 us
  waiting for transfers between devices: 129 us -> 0 us
  Pallas kernels: 0 us -> 54.4 us
  matrix products: 22.2 us -> 0 us
  other arithmetic: 20.3 us -> 0 us
  starting transfers between devices: 18.4 us -> 0 us
  between operations: 13.5 us -> 0.01 us
  local copies, waits for them, and re-layouts: 7.31 us -> 3.88 us
    ppermute x9 -> x0, waiting for transfers between devices: 76.7 us -> none  [shifted(): lax.ppermute(value, axis, [(source, source + steps) for source in range(l...]
    pallas_call x0 -> x1, Pallas kernels: none -> 54.4 us  [on_device(): pl.pallas_call(functools.partial(layer_kernel, n_ctx, n_tp, chunk), out_s...]
    reduce_scatter x1 -> x0, waiting for transfers between devices: 51.9 us -> none  [on_device(): lax.psum_scatter(jnp.dot(normed, out_weight, preferred_element_type=jnp.f...]
    dot_general x6 -> x0, matrix products: 22.2 us -> none  [the longest x1 10 us: on_device(): jnp.dot(normed, out_weight, preferred_element_type=jnp.float32)]
    ppermute x9 -> x0, starting transfers between devices: 18.4 us -> none  [shifted(): lax.ppermute(value, axis, [(source, source + steps) for source in range(l...]
    add x7 -> x0, other arithmetic: 7.16 us -> none  [relay_turn(): return (incoming, block_decay[:, None, None] * incoming + local_state)]
    convert_element_type x2 -> x0, other arithmetic: 5.8 us -> none  [the longest x1 3.89 us: on_device(): x_conv = jax.nn.silu(causal_conv(jnp.concatenate([prev_x, x_inputs], 0),...]
    unnamed x19 -> x2, local copies, waits for them, and re-layouts: 1.52 us -> 3.88 us
  transfers between devices with their start and end apart: 10 -> 0, of which waited for: 8 -> 0; matrix products, arithmetic and copies ran while one was open for 6% -> 0% of each run, Pallas kernels for 0% -> 0%
where the time goes in v1:
time: 58.6 us; the launch traced here: 58.3 us
  Pallas kernels  54.4 us (93%)
  local copies, waits for them, and re-layouts  3.88 us (7%)
    pallas_call x1, Pallas kernels, on_device(): pl.pallas_call(functools.partial(layer_kernel, n_ctx, n_tp, chunk), out_s...  54.4 us
    unnamed x2, local copies, waits for them, and re-layouts  3.88 us

profile of v1, /device:TPU:25, one launch (start us, length us, event | category | flops | bytes accessed | tf_op | source)
XLA Modules:
  0.0 58.3 jit_solution(16190946166393175214)
XLA Ops:
  0.0 1.6 %copy.12.step_ref = f32[512,16]{1,0:T(8,128)} copy(f32[512,16]{0,1:T(8,128)} %param.14) | data formatting | bytes 65536 | tf_op args[3]
  1.6 54.4 %layer.1 = bf16[128,4096]{1,0:T(8,128)(2,1)} custom-call(bf16[512,1024]{1,0:T(8,128)(2,1)} %x_ref.1, bf16[512,256]{1,0:T(8,128)(2,1)} %m_ref.1, bf16[512,1024]{1,0:T(8,128)(2,1)} %z_ref.1, f32[512,16]{1,0:T(8,128)} %copy.12.step_ref, f32[1,16]{1,0:T(1,128)} %bitcast.5, f32[1,16]{1,0:T(1,128)} %bitcast.6, f32[1,16]{1,0:T(1,128)} %bitcast.7, ...), custom_call_target="tpu_custom_call" | custom-call | flops 5368709120 | bytes 16777216 | tf_op jit(solution)/shard_map/layer/pallas_call | solution.py:389
  56.0 2.3 %copy.14 = bf16[128,4096]{1,0:T(8,128)(2,1)} copy(bf16[128,4096]{1,0:T(8,128)(2,1)} %layer.1) | data formatting | bytes 2097152

commit v2 on v1

--- a/solution.py
+++ b/solution.py
@@ -22,15 +22,15 @@
     x_ref, m_ref, z_ref, step_ref, bias_ref, decay_ref, skip_ref, xf_ref, mf_ref, gain_ref, w_hbm,
     out_ref,
     w_ref, hx_ref, hm_ref, pad_ref, xfs_ref, mfs_ref, gains_ref, skips_ref,
-    col_ref, sq_ref, at_ref, rt_ref, aexp_ref, dsend_ref, drecv_ref,
+    sq_ref, parts_ref, left_ref, right_ref, dsend_ref, drecv_ref,
     xc_ref, bt_ref, c_ref, cb_ref, lown_ref, lsend_ref, lrecv_ref, csend_ref, crecv_ref, sr_ref,
-    yg_ref, eg_ref, gated_ref, normed_ref, part_ref, core_ref, ysend_ref, yrecv_ref,
-    w_sem, halo_send, halo_recv, dec_send, dec_recv, pair_send, pair_recv, chain_send, chain_recv,
+    yg_ref, eg_ref, gated_ref, normed_ref, part_ref, core_ref, ysend_ref, yrecv_ref, out_buf,
+    w_sem, out_sem, halo_send, halo_recv, dec_send, dec_recv, pair_send, pair_recv, chain_send, chain_recv,
     core_send, core_recv, y_send, y_recv,
 ):
     length = x_ref.shape[0]
     pairs = x_ref.shape[1] // LANES
-    heads = step_ref.shape[1]
+    heads = step_ref.shape[0]
     n_y = n_tp // 2
     rows = length // n_tp
     n_chunks = w_hbm.shape[1] // chunk
@@ -53,12 +53,42 @@
         pl.semaphore_signal(
             barrier, inc=1, device_id={"tp": ((y + off) % n_y) * 2 + core}, device_id_type=MESH
         )
-    pl.semaphore_wait(barrier, 4 + 1 + (n_y - 1))
 
     def remote(src, dst, send, recv, where):
         return pltpu.make_async_remote_copy(
             src_ref=src, dst_ref=dst, send_sem=send, recv_sem=recv, device_id=where, device_id_type=MESH
         )
+
+    def lane_column(ref):
+        sq_ref[...] = jnp.zeros_like(sq_ref)
+        sq_ref[:, :heads] = jnp.broadcast_to(ref[...], (LANES, heads))
+        return sq_ref[...].T
+
+    def three_terms(v):
+        first = v.astype(jnp.bfloat16).astype(jnp.float32)
+        second = (v - first).astype(jnp.bfloat16).astype(jnp.float32)
+        return [first, second, (v - first - second).astype(jnp.bfloat16).astype(jnp.float32)]
+
+    def all_tokens(column):
+        return jnp.concatenate([column[:heads]] * (length // LANES), axis=1)
+
+    step = jnp.log(1.0 + jnp.exp(step_ref[...] + all_tokens(lane_column(bias_ref))))
+    rate = step * jnp.exp(all_tokens(lane_column(decay_ref)))
+    skip_t = lane_column(skip_ref)
+    s_ids = lax.broadcasted_iota(jnp.int32, (length, length), 0)
+    t_ids = lax.broadcasted_iota(jnp.int32, (length, length), 1)
+    upper = jnp.where(s_ids <= t_ids, 1.0, 0.0).astype(jnp.bfloat16)
+    sums = jnp.dot(
+        jnp.concatenate(three_terms(rate), axis=0).astype(jnp.bfloat16), upper,
+        preferred_element_type=jnp.float32,
+    )
+    sums = sums[:heads] + sums[heads : 2 * heads] + sums[2 * heads :]
+    source = sums + jnp.log(step)
+    filler = jnp.ones((LANES - 6 * heads, length), jnp.float32)
+    parts_ref[...] = jnp.concatenate(three_terms(sums) + three_terms(source) + [filler], axis=0)
+    left_ref[...] = parts_ref[...].T.astype(jnp.bfloat16)
+
+    pl.semaphore_wait(barrier, 4 + 1 + (n_y - 1))
 
     following = {"ctx": (ctx + 1) % n_ctx}
     halo_x = remote(x_ref.at[pl.ds(length - HALO, HALO)], hx_ref, halo_send.at[0], halo_recv.at[0], following)
@@ -66,21 +96,6 @@
     halo_m.start()
     halo_x.start()
 
-    step = jnp.log(1.0 + jnp.exp(step_ref[...] + bias_ref[...]))
-    col_ref[...] = jnp.zeros_like(col_ref)
-    col_ref[:, :heads] = step * jnp.exp(decay_ref[...])
-    rate_t = col_ref[...].T[:heads]
-    col_ref[:, :heads] = jnp.log(step)
-    log_step_t = col_ref[...].T[:heads]
-    s_ids = lax.broadcasted_iota(jnp.int32, (length, length), 0)
-    t_ids = lax.broadcasted_iota(jnp.int32, (length, length), 1)
-    upper = jnp.where(s_ids <= t_ids, 1.0, 0.0).astype(jnp.float32)
-    sums = jnp.dot(rate_t, upper, precision=lax.Precision.HIGHEST, preferred_element_type=jnp.float32)
-    at_ref[...] = sums
-    rt_ref[...] = sums + log_step_t
-    sq_ref[...] = jnp.zeros_like(sq_ref)
-    sq_ref[:, :heads] = jnp.broadcast_to(skip_ref[...], (LANES, heads))
-    skip_t = sq_ref[...].T
     lane_row = lax.broadcasted_iota(jnp.int32, (1, LANES), 1) < LANES // 2
     x_taps = xf_ref[...].astype(jnp.float32)
     m_taps = mf_ref[...].astype(jnp.float32)
@@ -93,15 +108,18 @@
     for p in range(2):
         mfs_ref[p] = m_taps[:, p * LANES : (p + 1) * LANES]
 
-    head_sub = lax.broadcasted_iota(jnp.int32, (LANES, length), 0) < LANES // 2
-
-    def by_pair(ref, p):
-        return jnp.where(head_sub, ref[pl.ds(2 * p, 1), :], ref[pl.ds(2 * p + 1, 1), :]).T
+    def picker(p, base):
+        row = lax.broadcasted_iota(jnp.int32, (LANES, LANES), 0) - base
+        head = 2 * p + (lax.broadcasted_iota(jnp.int32, (LANES, LANES), 1) >= LANES // 2).astype(jnp.int32)
+        hit = (row == head) | (row == head + heads) | (row == head + 2 * heads)
+        return jnp.where(hit, 1.0, 0.0).astype(jnp.bfloat16)
+
+    def by_pair(start, p, base):
+        return jnp.dot(left_ref[start:, :], picker(p, base), preferred_element_type=jnp.float32)
 
     def expand(p, _):
-        spread = by_pair(at_ref, p)
-        aexp_ref[p] = spread
-        dsend_ref[p] = jnp.broadcast_to(spread[length - 1 : length], (8, LANES))
+        last = by_pair(length - HALO, p, 0)
+        dsend_ref[p] = jnp.broadcast_to(last[HALO - 1 :], (8, LANES))
         return 0
 
     lax.fori_loop(0, pairs, expand, 0)
@@ -128,19 +146,16 @@
     def pair_copy(p):
         return remote(lsend_ref.at[p], lrecv_ref.at[p], pair_send.at[p], pair_recv.at[p], {"ctx": mate})
 
-    def local_state(p, _):
+    def local_state(p):
         cols = pl.ds(pl.multiple_of(p * LANES, LANES), LANES)
         xc = conv(x_ref[:, cols], hx_ref[:, cols], xfs_ref[p]).astype(jnp.bfloat16)
         xc_ref[p] = xc
-        tail = jnp.exp(by_pair(rt_ref, p) - dsend_ref[p][0:1])
+        tail = jnp.exp(by_pair(0, p, 3 * heads) - dsend_ref[p][0:1])
         u = (tail * xc.astype(jnp.float32)).astype(jnp.bfloat16)
         state = jnp.dot(bt_ref[...], u, preferred_element_type=jnp.float32)
         lown_ref[p] = state
         lsend_ref[p] = state.astype(jnp.bfloat16)
         pair_copy(p).start()
-        return 0
-
-    lax.fori_loop(0, pairs, local_state, 0)
 
     scores = jnp.dot(c_ref[...], bt_ref[...], preferred_element_type=jnp.float32)
     cb_ref[...] = jnp.where(s_ids >= t_ids, scores, 0.0)
@@ -185,16 +200,25 @@
     half = length // 2
     low_lanes = lax.broadcasted_iota(jnp.int32, (half, LANES), 1) < LANES // 2
 
+    row_ids = lax.broadcasted_iota(jnp.int32, (LANES, length), 0)
+
     def within(p):
         xc = xc_ref[p]
         tops, bottoms = [], []
         for h in range(2):
-            row_r = rt_ref[pl.ds(2 * p + h, 1), :]
-            col_a = jnp.broadcast_to(at_ref[pl.ds(2 * p + h, 1), :], (LANES, length)).T
-            col_a = jnp.concatenate([col_a] * (half // LANES), axis=1)
+            head = 2 * p + h
+            hit = (row_ids == head) | (row_ids == head + heads) | (row_ids == head + 2 * heads)
+            right = jnp.where(hit, -1.0, 0.0)
+            for term in range(3):
+                row = parts_ref[pl.ds((3 + term) * heads + head, 1), :]
+                right = jnp.where(row_ids == 6 * heads + term, row, right)
+            right_ref[...] = right.astype(jnp.bfloat16)
 
             def weigh(t0, s0, masked):
-                power = row_r[:, s0 : s0 + half] - col_a[t0 : t0 + half]
+                power = jnp.dot(
+                    left_ref[t0 : t0 + half, :], right_ref[:, s0 : s0 + half],
+                    preferred_element_type=jnp.float32,
+                )
                 if masked:
                     power = jnp.minimum(power, 64.0)
                 return (jnp.exp(power) * cb_ref[t0 : t0 + half, s0 : s0 + half]).astype(jnp.bfloat16)
@@ -206,14 +230,15 @@
             )
         cols = pl.ds(pl.multiple_of(p * LANES, LANES), LANES)
         skip = skips_ref[p][0:1]
+        decay = jnp.exp(-by_pair(0, p, 0))
         for t0, both in ((0, tops), (half, bottoms)):
             here = pl.ds(t0, half)
             gate = half_silu(z_ref[here, cols].astype(jnp.float32))
             own = jnp.where(low_lanes, both[0], both[1])
             yg_ref[p, here] = (own + skip * xc[t0 : t0 + half].astype(jnp.float32)) * gate
-            eg_ref[p, here] = jnp.exp(-aexp_ref[p, here]) * gate
-
-    lag = jnp.minimum(2 * z, pairs)
+            eg_ref[p, here] = decay[t0 : t0 + half] * gate
+
+    lag = jnp.minimum(3 + 3 * z, 2 * pairs)
 
     def turn(i, _):
         @pl.when((i >= lag) & (i < lag + pairs))
@@ -222,11 +247,15 @@
 
         @pl.when(i < pairs)
         def _():
-            within(i)
+            local_state(i)
+
+        @pl.when((i >= pairs) & (i < 2 * pairs))
+        def _():
+            within(i - pairs)
 
         return 0
 
-    lax.fori_loop(0, 2 * pairs, turn, 0)
+    lax.fori_loop(0, 3 * pairs, turn, 0)
 
     span = 2 * rows
     channels = x_ref.shape[1]
@@ -296,13 +325,17 @@
         if slot > 0:
             forward(n_chunks - 1)
 
+    def out_copy(k):
+        cols = pl.ds(pl.multiple_of(k * chunk, chunk), chunk)
+        return pltpu.make_async_copy(out_buf.at[k], out_ref.at[:, cols], out_sem.at[k])
+
     def finish(k, _):
         total = chip_sum(0, k)
         for slot in range(1, n_y):
             y_copy(slot, k).wait_recv()
             total = total + yrecv_ref[slot - 1, k].astype(jnp.float32)
-        cols = pl.ds(pl.multiple_of(k * chunk, chunk), chunk)
-        out_ref[:, cols] = total.astype(jnp.bfloat16)
+        out_buf[k] = total.astype(jnp.bfloat16)
+        out_copy(k).start()
         return 0
 
     lax.fori_loop(0, n_chunks, finish, 0)
@@ -323,6 +356,7 @@
     lax.fori_loop(0, pairs, drain_states, 0)
 
     def drain_parts(k, _):
+        out_copy(k).wait()
         for slot in range(n_y):
             core_copy(slot, k).wait_send()
         for slot in range(1, n_y):
@@ -356,11 +390,10 @@
         pltpu.VMEM((2, x_filter.shape[0], LANES), f32),
         pltpu.VMEM((pairs, 8, LANES), f32),
         pltpu.VMEM((pairs, 8, LANES), f32),
-        pltpu.VMEM((length, LANES), f32),
         pltpu.VMEM((LANES, LANES), f32),
-        pltpu.VMEM((heads, length), f32),
-        pltpu.VMEM((heads, length), f32),
-        pltpu.VMEM((pairs, length, LANES), f32),
+        pltpu.VMEM((LANES, length), f32),
+        pltpu.VMEM((length, LANES), bf16),
+        pltpu.VMEM((LANES, length), bf16),
         pltpu.VMEM((pairs, 8, LANES), f32),
         pltpu.VMEM((pairs, 8, LANES), f32),
         pltpu.VMEM((pairs, length, LANES), bf16),
@@ -381,7 +414,8 @@
         pltpu.VMEM((n_y, n_chunks, rows, chunk), bf16),
         pltpu.VMEM((n_y - 1, n_chunks, rows, chunk), bf16),
         pltpu.VMEM((n_y - 1, n_chunks, rows, chunk), bf16),
-        dma, dma((2,)), dma((2,)), dma, dma,
+        pltpu.VMEM((n_chunks, rows, chunk), bf16),
+        dma, dma((n_chunks,)), dma((2,)), dma((2,)), dma, dma,
         dma((pairs,)), dma((pairs,)), dma((pairs,)), dma((pairs,)),
         dma((n_y, n_chunks)), dma((n_y, n_chunks)),
         dma((n_y - 1, n_chunks)), dma((n_y - 1, n_chunks)),
@@ -390,7 +424,7 @@
         functools.partial(layer_kernel, n_ctx, n_tp, chunk),
         out_shape=jax.ShapeDtypeStruct((rows, model), bf16),
         in_specs=[vmem] * 10 + [pl.BlockSpec(memory_space=pl.ANY)],
-        out_specs=vmem,
+        out_specs=pl.BlockSpec(memory_space=pl.ANY),
         scratch_shapes=scratch,
         compiler_params=pltpu.CompilerParams(
             collective_id=0, has_side_effects=True, vmem_limit_bytes=58 * 1024 * 1024
@@ -401,7 +435,7 @@
         ),
         name="layer",
     )(
-        x_inputs, state_maps, z_gate, step_raw, step_bias[None], decay_log[None], skip_gain[None],
+        x_inputs, state_maps, z_gate, step_raw.T, step_bias[None], decay_log[None], skip_gain[None],
         x_filter, state_filter, norm_gain[None], out_weight,
     )
 

time: 58.6 us -> 61.4 us (1.048)
  Pallas kernels: 54.4 us -> 58.3 us
  local copies, waits for them, and re-layouts: 3.88 us -> 2.29 us
    pallas_call x1, Pallas kernels: 54.4 us -> 58.3 us  [on_device(): pl.pallas_call(functools.partial(layer_kernel, n_ctx, n_tp, chunk), out_s...]
    unnamed x2 -> x1, local copies, waits for them, and re-layouts: 3.88 us -> 2.29 us
where the time goes in v2:
time: 61.4 us; the launch traced here: 60.6 us
  Pallas kernels  58.3 us (95%)
  local copies, waits for them, and re-layouts  2.29 us (4%)
    pallas_call x1, Pallas kernels, on_device(): pl.pallas_call(functools.partial(layer_kernel, n_ctx, n_tp, chunk), out_s...  58.3 us
    unnamed x1, local copies, waits for them, and re-layouts  2.29 us

profile of v2, /device:TPU:25, one launch (start us, length us, event | category | flops | bytes accessed | tf_op | source)
XLA Modules:
  0.0 60.6 jit_solution(13111084893344622020)
XLA Ops:
  0.0 58.3 %layer.1 = bf16[128,4096]{1,0:T(8,128)(2,1)} custom-call(bf16[512,1024]{1,0:T(8,128)(2,1)} %x_ref.1, bf16[512,256]{1,0:T(8,128)(2,1)} %m_ref.1, bf16[512,1024]{1,0:T(8,128)(2,1)} %z_ref.1, f32[16,512]{1,0:T(8,128)} %bitcast.5, f32[1,16]{1,0:T(1,128)} %bitcast.7, f32[1,16]{1,0:T(1,128)} %bitcast.8, f32[1,16]{1,0:T(1,128)} %bitcast.9, bf16[4,1024]{1,0:T(4,128)(2,1)} %xf_ref.1, ...), custom_call_target="tpu_custom_call" | custom-call | flops 5368709120 | bytes 16777216 | tf_op jit(solution)/shard_map/layer/pallas_call | solution.py:423
  58.3 2.3 %copy.13 = bf16[128,4096]{1,0:T(8,128)(2,1)} copy(bf16[128,4096]{1,0:T(8,128)(2,1)} %layer.1) | data formatting | bytes 2097152

commit v3 on v2

--- a/solution.py
+++ b/solution.py
@@ -22,8 +22,8 @@
     x_ref, m_ref, z_ref, step_ref, bias_ref, decay_ref, skip_ref, xf_ref, mf_ref, gain_ref, w_hbm,
     out_ref,
     w_ref, hx_ref, hm_ref, pad_ref, xfs_ref, mfs_ref, gains_ref, skips_ref,
-    sq_ref, parts_ref, left_ref, right_ref, dsend_ref, drecv_ref,
-    xc_ref, bt_ref, c_ref, cb_ref, lown_ref, lsend_ref, lrecv_ref, csend_ref, crecv_ref, sr_ref,
+    sq_ref, parts_ref, left_ref, pick_ref, dsend_ref, drecv_ref,
+    xc_ref, uc_ref, aexp_ref, mid_ref, first_ref, bt_ref, c_ref, cb_ref, lown_ref, lsend_ref, lrecv_ref, csend_ref, crecv_ref, sr_ref,
     yg_ref, eg_ref, gated_ref, normed_ref, part_ref, core_ref, ysend_ref, yrecv_ref, out_buf,
     w_sem, out_sem, halo_send, halo_recv, dec_send, dec_recv, pair_send, pair_recv, chain_send, chain_recv,
     core_send, core_recv, y_send, y_recv,
@@ -108,57 +108,75 @@
     for p in range(2):
         mfs_ref[p] = m_taps[:, p * LANES : (p + 1) * LANES]
 
-    def picker(p, base):
-        row = lax.broadcasted_iota(jnp.int32, (LANES, LANES), 0) - base
-        head = 2 * p + (lax.broadcasted_iota(jnp.int32, (LANES, LANES), 1) >= LANES // 2).astype(jnp.int32)
-        hit = (row == head) | (row == head + heads) | (row == head + 2 * heads)
-        return jnp.where(hit, 1.0, 0.0).astype(jnp.bfloat16)
-
-    def by_pair(start, p, base):
-        return jnp.dot(left_ref[start:, :], picker(p, base), preferred_element_type=jnp.float32)
-
-    def expand(p, _):
-        last = by_pair(length - HALO, p, 0)
-        dsend_ref[p] = jnp.broadcast_to(last[HALO - 1 :], (8, LANES))
-        return 0
-
-    lax.fori_loop(0, pairs, expand, 0)
+    channels = x_ref.shape[1]
+    term = lax.broadcasted_iota(jnp.int32, (LANES, channels), 0)
+    owner = lax.broadcasted_iota(jnp.int32, (LANES, channels), 1) // (channels // heads)
+    match = term % heads == owner
+    pick_sum = jnp.where(match & (term < 3 * heads), 1.0, 0.0).astype(jnp.bfloat16)
+    pick_source = jnp.where(match & (term >= 3 * heads) & (term < 6 * heads), 1.0, 0.0).astype(jnp.bfloat16)
+    last = jnp.dot(left_ref[length - HALO :, :], pick_sum, preferred_element_type=jnp.float32)[HALO - 1 :]
+    for p in range(pairs):
+        cols = slice(p * LANES, (p + 1) * LANES)
+        pick_ref[p, :, :LANES] = pick_sum[:, cols]
+        pick_ref[p, :, LANES:] = pick_source[:, cols]
+        dsend_ref[p] = jnp.broadcast_to(last[:, cols], (8, LANES))
     dec_copy = remote(dsend_ref, drecv_ref, dec_send, dec_recv, {"ctx": mate})
     dec_copy.start()
 
     taps = xf_ref.shape[0]
     has_prev = jnp.where(ctx > 0, 1.0, 0.0).astype(jnp.float32)
 
-    def conv(block, halo, filters):
-        pad_ref[0:8] = halo.astype(jnp.float32)[HALO - 8 :] * has_prev
-        pad_ref[8:] = block.astype(jnp.float32)
-        total = filters[0:1] * pad_ref[9 - taps : 9 - taps + length]
+    def conv(block, halo, filters, slot):
+        pad_ref[slot, 0:8] = halo.astype(jnp.float32)[HALO - 8 :] * has_prev
+        pad_ref[slot, 8:] = block.astype(jnp.float32)
+        total = filters[0:1] * pad_ref[slot, 9 - taps : 9 - taps + length]
         for k in range(1, taps):
             start = 9 - taps + k
-            total = total + filters[k : k + 1] * pad_ref[start : start + length]
+            total = total + filters[k : k + 1] * pad_ref[slot, start : start + length]
         return half_silu(total)
 
     halo_m.wait_recv()
-    bt_ref[...] = conv(m_ref[:, :LANES], hm_ref[:, :LANES], mfs_ref[0]).T.astype(jnp.bfloat16)
-    c_ref[...] = conv(m_ref[:, LANES:], hm_ref[:, LANES:], mfs_ref[1]).astype(jnp.bfloat16)
+    bt_ref[...] = conv(m_ref[:, :LANES], hm_ref[:, :LANES], mfs_ref[0], 0).T.astype(jnp.bfloat16)
+    c_ref[...] = conv(m_ref[:, LANES:], hm_ref[:, LANES:], mfs_ref[1], 1).astype(jnp.bfloat16)
     halo_x.wait_recv()
 
     def pair_copy(p):
         return remote(lsend_ref.at[p], lrecv_ref.at[p], pair_send.at[p], pair_recv.at[p], {"ctx": mate})
 
-    def local_state(p):
+    half = length // 2
+
+    def local_state(p, slot):
         cols = pl.ds(pl.multiple_of(p * LANES, LANES), LANES)
-        xc = conv(x_ref[:, cols], hx_ref[:, cols], xfs_ref[p]).astype(jnp.bfloat16)
+        xc = conv(x_ref[:, cols], hx_ref[:, cols], xfs_ref[p], slot).astype(jnp.bfloat16)
         xc_ref[p] = xc
-        tail = jnp.exp(by_pair(0, p, 3 * heads) - dsend_ref[p][0:1])
-        u = (tail * xc.astype(jnp.float32)).astype(jnp.bfloat16)
-        state = jnp.dot(bt_ref[...], u, preferred_element_type=jnp.float32)
+        both = jnp.dot(left_ref[...], pick_ref[p], preferred_element_type=jnp.float32)
+        sums, source = both[:, :LANES], both[:, LANES:]
+        aexp_ref[p] = sums
+        wide = xc.astype(jnp.float32)
+        end = dsend_ref[p][0:1]
+        border = sums[half - 1 : half]
+        mids, states = [], []
+        for j, stop in ((0, border), (1, end)):
+            here = slice(j * half, (j + 1) * half)
+            mid = sums[j * half + half // 2 - 1 : j * half + half // 2]
+            mid_ref[p, j] = jnp.broadcast_to(mid, (8, LANES))
+            u = (jnp.exp(source[here] - mid) * wide[here]).astype(jnp.bfloat16)
+            uc_ref[p, here] = u
+            fresh = jnp.dot(bt_ref[:, here], u, preferred_element_type=jnp.float32)
+            mids.append(mid)
+            states.append(fresh * jnp.exp(mid - stop))
+        first_ref[p] = (states[0] * jnp.exp(border - mids[1])).astype(jnp.bfloat16)
+        state = states[0] * jnp.exp(border - end) + states[1]
         lown_ref[p] = state
         lsend_ref[p] = state.astype(jnp.bfloat16)
         pair_copy(p).start()
 
-    scores = jnp.dot(c_ref[...], bt_ref[...], preferred_element_type=jnp.float32)
-    cb_ref[...] = jnp.where(s_ids >= t_ids, scores, 0.0)
+    row_half = lax.broadcasted_iota(jnp.int32, (half, half), 0)
+    col_half = lax.broadcasted_iota(jnp.int32, (half, half), 1)
+    for j in range(2):
+        here = slice(j * half, (j + 1) * half)
+        scores = jnp.dot(c_ref[here, :], bt_ref[:, here], preferred_element_type=jnp.float32)
+        cb_ref[j] = jnp.where(row_half >= col_half, scores, 0.0).astype(jnp.bfloat16)
 
     is_odd = odd.astype(jnp.float32)
     is_even = 1.0 - is_odd
@@ -197,68 +215,44 @@
             csend_ref[p] = (d_odd * middle + l_odd).astype(jnp.bfloat16)
             chain_copy(p).start()
 
-    half = length // 2
-    low_lanes = lax.broadcasted_iota(jnp.int32, (half, LANES), 1) < LANES // 2
-
-    row_ids = lax.broadcasted_iota(jnp.int32, (LANES, length), 0)
-
     def within(p):
-        xc = xc_ref[p]
-        tops, bottoms = [], []
-        for h in range(2):
-            head = 2 * p + h
-            hit = (row_ids == head) | (row_ids == head + heads) | (row_ids == head + 2 * heads)
-            right = jnp.where(hit, -1.0, 0.0)
-            for term in range(3):
-                row = parts_ref[pl.ds((3 + term) * heads + head, 1), :]
-                right = jnp.where(row_ids == 6 * heads + term, row, right)
-            right_ref[...] = right.astype(jnp.bfloat16)
-
-            def weigh(t0, s0, masked):
-                power = jnp.dot(
-                    left_ref[t0 : t0 + half, :], right_ref[:, s0 : s0 + half],
-                    preferred_element_type=jnp.float32,
-                )
-                if masked:
-                    power = jnp.minimum(power, 64.0)
-                return (jnp.exp(power) * cb_ref[t0 : t0 + half, s0 : s0 + half]).astype(jnp.bfloat16)
-
-            tops.append(jnp.dot(weigh(0, 0, True), xc[:half], preferred_element_type=jnp.float32))
-            bottoms.append(
-                jnp.dot(weigh(half, 0, False), xc[:half], preferred_element_type=jnp.float32)
-                + jnp.dot(weigh(half, half, True), xc[half:], preferred_element_type=jnp.float32)
-            )
         cols = pl.ds(pl.multiple_of(p * LANES, LANES), LANES)
         skip = skips_ref[p][0:1]
-        decay = jnp.exp(-by_pair(0, p, 0))
-        for t0, both in ((0, tops), (half, bottoms)):
-            here = pl.ds(t0, half)
+        for j in range(2):
+            here = slice(j * half, (j + 1) * half)
+            own = jnp.dot(cb_ref[j], uc_ref[p, here], preferred_element_type=jnp.float32)
+            if j == 1:
+                own = own + jnp.dot(c_ref[here, :], first_ref[p], preferred_element_type=jnp.float32)
+            mid = mid_ref[p, j][0:1]
+            decay = jnp.exp(mid - aexp_ref[p, here])
             gate = half_silu(z_ref[here, cols].astype(jnp.float32))
-            own = jnp.where(low_lanes, both[0], both[1])
-            yg_ref[p, here] = (own + skip * xc[t0 : t0 + half].astype(jnp.float32)) * gate
-            eg_ref[p, here] = decay[t0 : t0 + half] * gate
-
-    lag = jnp.minimum(3 + 3 * z, 2 * pairs)
+            yg_ref[p, here] = (decay * own + skip * xc_ref[p, here].astype(jnp.float32)) * gate
+            eg_ref[p, here] = decay * jnp.exp(-mid) * gate
+
+    twos = pairs // 2
+    lag = jnp.minimum(2 + 2 * z, 2 * twos)
 
     def turn(i, _):
-        @pl.when((i >= lag) & (i < lag + pairs))
-        def _():
-            relay(i - lag)
-
-        @pl.when(i < pairs)
-        def _():
-            local_state(i)
-
-        @pl.when((i >= pairs) & (i < 2 * pairs))
-        def _():
-            within(i - pairs)
+        @pl.when((i >= lag) & (i < lag + twos))
+        def _():
+            for slot in range(2):
+                relay(2 * (i - lag) + slot)
+
+        @pl.when(i < twos)
+        def _():
+            for slot in range(2):
+                local_state(2 * i + slot, slot)
+
+        @pl.when((i >= twos) & (i < 2 * twos))
+        def _():
+            for slot in range(2):
+                within(2 * (i - twos) + slot)
 
         return 0
 
-    lax.fori_loop(0, 3 * pairs, turn, 0)
+    lax.fori_loop(0, 3 * twos, turn, 0)
 
     span = 2 * rows
-    channels = x_ref.shape[1]
 
     def project_rows(first):
         here = pl.ds(pl.multiple_of(first, span), span)
@@ -385,7 +379,7 @@
         pltpu.VMEM(out_weight.shape, bf16),
         pltpu.VMEM((HALO, channels), bf16),
         pltpu.VMEM((HALO, 2 * state), bf16),
-        pltpu.VMEM((length + 8, LANES), f32),
+        pltpu.VMEM((2, length + 8, LANES), f32),
         pltpu.VMEM((pairs, x_filter.shape[0], LANES), f32),
         pltpu.VMEM((2, x_filter.shape[0], LANES), f32),
         pltpu.VMEM((pairs, 8, LANES), f32),
@@ -393,13 +387,17 @@
         pltpu.VMEM((LANES, LANES), f32),
         pltpu.VMEM((LANES, length), f32),
         pltpu.VMEM((length, LANES), bf16),
-        pltpu.VMEM((LANES, length), bf16),
+        pltpu.VMEM((pairs, LANES, 2 * LANES), bf16),
         pltpu.VMEM((pairs, 8, LANES), f32),
         pltpu.VMEM((pairs, 8, LANES), f32),
         pltpu.VMEM((pairs, length, LANES), bf16),
+        pltpu.VMEM((pairs, length, LANES), bf16),
+        pltpu.VMEM((pairs, length, LANES), f32),
+        pltpu.VMEM((pairs, 2, 8, LANES), f32),
+        pltpu.VMEM((pairs, state, LANES), bf16),
         pltpu.VMEM((state, length), bf16),
         pltpu.VMEM((length, state), bf16),
-        pltpu.VMEM((length, length), f32),
+        pltpu.VMEM((2, length // 2, length // 2), bf16),
         pltpu.VMEM((pairs, state, LANES), f32),
         pltpu.VMEM((pairs, state, LANES), bf16),
         pltpu.VMEM((pairs, state, LANES), bf16),

time: 61.4 us -> 57.5 us (0.936)
  Pallas kernels: 58.3 us -> 54.7 us
    pallas_call x1, Pallas kernels: 58.3 us -> 54.7 us  [on_device(): pl.pallas_call(functools.partial(layer_kernel, n_ctx, n_tp, chunk), out_s...]
where the time goes in v3:
time: 57.5 us; the launch traced here: 57 us
  Pallas kernels  54.7 us (95%)
  local copies, waits for them, and re-layouts  2.29 us (4%)
    pallas_call x1, Pallas kernels, on_device(): pl.pallas_call(functools.partial(layer_kernel, n_ctx, n_tp, chunk), out_s...  54.7 us
    unnamed x1, local copies, waits for them, and re-layouts  2.29 us

profile of v3, /device:TPU:25, one launch (start us, length us, event | category | flops | bytes accessed | tf_op | source)
XLA Modules:
  0.0 57.0 jit_solution(15980172183064092840)
XLA Ops:
  0.0 54.7 %layer.1 = bf16[128,4096]{1,0:T(8,128)(2,1)} custom-call(bf16[512,1024]{1,0:T(8,128)(2,1)} %x_ref.1, bf16[512,256]{1,0:T(8,128)(2,1)} %m_ref.1, bf16[512,1024]{1,0:T(8,128)(2,1)} %z_ref.1, f32[16,512]{1,0:T(8,128)} %bitcast.5, f32[1,16]{1,0:T(1,128)} %bitcast.7, f32[1,16]{1,0:T(1,128)} %bitcast.8, f32[1,16]{1,0:T(1,128)} %bitcast.9, bf16[4,1024]{1,0:T(4,128)(2,1)} %xf_ref.1, ...), custom_call_target="tpu_custom_call" | custom-call | flops 5368709120 | bytes 16777216 | tf_op jit(solution)/shard_map/layer/pallas_call | solution.py:421
  54.7 2.3 %copy.13 = bf16[128,4096]{1,0:T(8,128)(2,1)} copy(bf16[128,4096]{1,0:T(8,128)(2,1)} %layer.1) | data formatting | bytes 2097152

commit v4 on v3

--- a/solution.py
+++ b/solution.py
@@ -19,13 +19,13 @@
 
 def layer_kernel(
     n_ctx, n_tp, chunk,
-    x_ref, m_ref, z_ref, step_ref, bias_ref, decay_ref, skip_ref, xf_ref, mf_ref, gain_ref, w_hbm,
+    x_hbm, m_hbm, z_hbm, step_ref, bias_ref, decay_ref, skip_ref, xf_ref, mf_ref, gain_ref, w_hbm,
     out_ref,
-    w_ref, hx_ref, hm_ref, pad_ref, xfs_ref, mfs_ref, gains_ref, skips_ref,
+    w_ref, x_ref, m_ref, z_ref, hx_ref, hm_ref, pad_ref, xfs_ref, mfs_ref, gains_ref, skips_ref,
     sq_ref, parts_ref, left_ref, pick_ref, dsend_ref, drecv_ref,
     xc_ref, uc_ref, aexp_ref, mid_ref, first_ref, bt_ref, c_ref, cb_ref, lown_ref, lsend_ref, lrecv_ref, csend_ref, crecv_ref, sr_ref,
     yg_ref, eg_ref, gated_ref, normed_ref, part_ref, core_ref, ysend_ref, yrecv_ref, out_buf,
-    w_sem, out_sem, halo_send, halo_recv, dec_send, dec_recv, pair_send, pair_recv, chain_send, chain_recv,
+    w_sem, in_sem, out_sem, halo_send, halo_recv, dec_send, dec_recv, pair_send, pair_recv, chain_send, chain_recv,
     core_send, core_recv, y_send, y_recv,
 ):
     length = x_ref.shape[0]
@@ -43,7 +43,9 @@
     other_core = y * 2 + 1 - core
 
     w_copy = pltpu.make_async_copy(w_hbm, w_ref, w_sem)
-    w_copy.start()
+    m_copy = pltpu.make_async_copy(m_hbm, m_ref, in_sem.at[0])
+    x_copy = pltpu.make_async_copy(x_hbm, x_ref, in_sem.at[1])
+    z_copy = pltpu.make_async_copy(z_hbm, z_ref, in_sem.at[2])
 
     barrier = pltpu.get_barrier_semaphore()
     for off in (1, n_ctx - 1, 2, n_ctx - 2):
@@ -54,6 +56,9 @@
             barrier, inc=1, device_id={"tp": ((y + off) % n_y) * 2 + core}, device_id_type=MESH
         )
 
+    for copy in (m_copy, x_copy, z_copy, w_copy):
+        copy.start()
+
     def remote(src, dst, send, recv, where):
         return pltpu.make_async_remote_copy(
             src_ref=src, dst_ref=dst, send_sem=send, recv_sem=recv, device_id=where, device_id_type=MESH
@@ -75,6 +80,15 @@
     step = jnp.log(1.0 + jnp.exp(step_ref[...] + all_tokens(lane_column(bias_ref))))
     rate = step * jnp.exp(all_tokens(lane_column(decay_ref)))
     skip_t = lane_column(skip_ref)
+
+    pl.semaphore_wait(barrier, 4 + 1 + (n_y - 1))
+
+    following = {"ctx": (ctx + 1) % n_ctx}
+    halo_x = remote(x_hbm.at[pl.ds(length - HALO, HALO)], hx_ref, halo_send.at[0], halo_recv.at[0], following)
+    halo_m = remote(m_hbm.at[pl.ds(length - HALO, HALO)], hm_ref, halo_send.at[1], halo_recv.at[1], following)
+    halo_m.start()
+    halo_x.start()
+
     s_ids = lax.broadcasted_iota(jnp.int32, (length, length), 0)
     t_ids = lax.broadcasted_iota(jnp.int32, (length, length), 1)
     upper = jnp.where(s_ids <= t_ids, 1.0, 0.0).astype(jnp.bfloat16)
@@ -88,14 +102,6 @@
     parts_ref[...] = jnp.concatenate(three_terms(sums) + three_terms(source) + [filler], axis=0)
     left_ref[...] = parts_ref[...].T.astype(jnp.bfloat16)
 
-    pl.semaphore_wait(barrier, 4 + 1 + (n_y - 1))
-
-    following = {"ctx": (ctx + 1) % n_ctx}
-    halo_x = remote(x_ref.at[pl.ds(length - HALO, HALO)], hx_ref, halo_send.at[0], halo_recv.at[0], following)
-    halo_m = remote(m_ref.at[pl.ds(length - HALO, HALO)], hm_ref, halo_send.at[1], halo_recv.at[1], following)
-    halo_m.start()
-    halo_x.start()
-
     lane_row = lax.broadcasted_iota(jnp.int32, (1, LANES), 1) < LANES // 2
     x_taps = xf_ref[...].astype(jnp.float32)
     m_taps = mf_ref[...].astype(jnp.float32)
@@ -110,8 +116,9 @@
 
     channels = x_ref.shape[1]
     term = lax.broadcasted_iota(jnp.int32, (LANES, channels), 0)
-    owner = lax.broadcasted_iota(jnp.int32, (LANES, channels), 1) // (channels // heads)
-    match = term % heads == owner
+    lane = lax.broadcasted_iota(jnp.int32, (LANES, channels), 1)
+    width = channels // heads
+    match = (lane >= (term & (heads - 1)) * width) & (lane < ((term & (heads - 1)) + 1) * width)
     pick_sum = jnp.where(match & (term < 3 * heads), 1.0, 0.0).astype(jnp.bfloat16)
     pick_source = jnp.where(match & (term >= 3 * heads) & (term < 6 * heads), 1.0, 0.0).astype(jnp.bfloat16)
     last = jnp.dot(left_ref[length - HALO :, :], pick_sum, preferred_element_type=jnp.float32)[HALO - 1 :]
@@ -135,9 +142,11 @@
             total = total + filters[k : k + 1] * pad_ref[slot, start : start + length]
         return half_silu(total)
 
+    m_copy.wait()
     halo_m.wait_recv()
     bt_ref[...] = conv(m_ref[:, :LANES], hm_ref[:, :LANES], mfs_ref[0], 0).T.astype(jnp.bfloat16)
     c_ref[...] = conv(m_ref[:, LANES:], hm_ref[:, LANES:], mfs_ref[1], 1).astype(jnp.bfloat16)
+    x_copy.wait()
     halo_x.wait_recv()
 
     def pair_copy(p):
@@ -229,6 +238,7 @@
             yg_ref[p, here] = (decay * own + skip * xc_ref[p, here].astype(jnp.float32)) * gate
             eg_ref[p, here] = decay * jnp.exp(-mid) * gate
 
+    z_copy.wait()
     twos = pairs // 2
     lag = jnp.minimum(2 + 2 * z, 2 * twos)
 
@@ -258,13 +268,12 @@
         here = pl.ds(pl.multiple_of(first, span), span)
         c_rows = c_ref[here, :]
 
-        def gate_pair(p, total):
+        squares = jnp.zeros((span, LANES), jnp.float32)
+        for p in range(pairs):
             inter = jnp.dot(c_rows, sr_ref[p], preferred_element_type=jnp.float32)
             gated = yg_ref[p, here] + eg_ref[p, here] * inter
             gated_ref[p] = gated
-            return total + gated * gated
-
-        squares = lax.fori_loop(0, pairs, gate_pair, jnp.zeros((span, LANES), jnp.float32))
+            squares = squares + gated * gated
         scale = lax.rsqrt(jnp.sum(squares, axis=1, keepdims=True) / channels + 1e-05)
         for p in range(pairs):
             normed_ref[:, p * LANES : (p + 1) * LANES] = (
@@ -374,9 +383,13 @@
     state = state_maps.shape[1] // 2
     bf16, f32 = jnp.bfloat16, jnp.float32
     vmem = pl.BlockSpec(memory_space=pltpu.VMEM)
+    anywhere = pl.BlockSpec(memory_space=pl.ANY)
     dma = pltpu.SemaphoreType.DMA
     scratch = [
         pltpu.VMEM(out_weight.shape, bf16),
+        pltpu.VMEM(x_inputs.shape, bf16),
+        pltpu.VMEM(state_maps.shape, bf16),
+        pltpu.VMEM(z_gate.shape, bf16),
         pltpu.VMEM((HALO, channels), bf16),
         pltpu.VMEM((HALO, 2 * state), bf16),
         pltpu.VMEM((2, length + 8, LANES), f32),
@@ -413,16 +426,16 @@
         pltpu.VMEM((n_y - 1, n_chunks, rows, chunk), bf16),
         pltpu.VMEM((n_y - 1, n_chunks, rows, chunk), bf16),
         pltpu.VMEM((n_chunks, rows, chunk), bf16),
-        dma, dma((n_chunks,)), dma((2,)), dma((2,)), dma, dma,
+        dma, dma((3,)), dma((n_chunks,)), dma((2,)), dma((2,)), dma, dma,
         dma((pairs,)), dma((pairs,)), dma((pairs,)), dma((pairs,)),
         dma((n_y, n_chunks)), dma((n_y, n_chunks)),
         dma((n_y - 1, n_chunks)), dma((n_y - 1, n_chunks)),
     ]
-    return pl.pallas_call(
+    mixed = pl.pallas_call(
         functools.partial(layer_kernel, n_ctx, n_tp, chunk),
         out_shape=jax.ShapeDtypeStruct((rows, model), bf16),
-        in_specs=[vmem] * 10 + [pl.BlockSpec(memory_space=pl.ANY)],
-        out_specs=pl.BlockSpec(memory_space=pl.ANY),
+        in_specs=[anywhere] * 3 + [vmem] * 7 + [anywhere],
+        out_specs=anywhere,
         scratch_shapes=scratch,
         compiler_params=pltpu.CompilerParams(
             collective_id=0, has_side_effects=True, vmem_limit_bytes=58 * 1024 * 1024
@@ -436,6 +449,26 @@
         x_inputs, state_maps, z_gate, step_raw.T, step_bias[None], decay_log[None], skip_gain[None],
         x_filter, state_filter, norm_gain[None], out_weight,
     )
+    return pl.pallas_call(
+        hand_over,
+        out_shape=jax.ShapeDtypeStruct((rows, model), bf16),
+        in_specs=[anywhere],
+        out_specs=anywhere,
+        scratch_shapes=[dma((4,))],
+        name="hand_over",
+    )(mixed)
+
+
+def hand_over(from_ref, to_ref, sems):
+    part = from_ref.shape[0] // 4
+    copies = [
+        pltpu.make_async_copy(from_ref.at[pl.ds(i * part, part)], to_ref.at[pl.ds(i * part, part)], sems.at[i])
+        for i in range(4)
+    ]
+    for copy in copies:
+        copy.start()
+    for copy in copies:
+        copy.wait()
 
 
 def solution(mesh):

time: 57.5 us -> 86.6 us (1.51)
  Pallas kernels: 54.7 us -> 86 us
  local copies, waits for them, and re-layouts: 2.29 us -> 0 us
    pallas_call x0 -> x1, Pallas kernels: none -> 32.9 us  [on_device(): pl.pallas_call(hand_over, out_shape=jax.ShapeDtypeStruct((rows, model), b...]
    unnamed x1 -> x0, local copies, waits for them, and re-layouts: 2.29 us -> none
    pallas_call x1, Pallas kernels: 54.7 us -> 53.1 us  [on_device(): pl.pallas_call(functools.partial(layer_kernel, n_ctx, n_tp, chunk), out_s...]
where the time goes in v4:
time: 86.6 us; the launch traced here: 86 us
  Pallas kernels  86 us (99%)
    pallas_call x1, Pallas kernels, on_device(): pl.pallas_call(functools.partial(layer_kernel, n_ctx, n_tp, chunk), out_s...  53.1 us
    pallas_call x1, Pallas kernels, on_device(): pl.pallas_call(hand_over, out_shape=jax.ShapeDtypeStruct((rows, model), b...  32.9 us

profile of v4, /device:TPU:25, one launch (start us, length us, event | category | flops | bytes accessed | tf_op | source)
XLA Modules:
  0.0 86.0 jit_solution(10637203082525047904)
XLA Ops:
  0.0 53.1 %layer.1.from_ref = bf16[128,4096]{1,0:T(8,128)(2,1)} custom-call(bf16[512,1024]{1,0:T(8,128)(2,1)} %x_hbm.1, bf16[512,256]{1,0:T(8,128)(2,1)} %m_hbm.1, bf16[512,1024]{1,0:T(8,128)(2,1)} %z_hbm.1, f32[16,512]{1,0:T(8,128)} %bitcast.5, f32[1,16]{1,0:T(1,128)} %bitcast.7, f32[1,16]{1,0:T(1,128)} %bitcast.8, f32[1,16]{1,0:T(1,128)} %bitcast.9, ...), custom_call_target="tpu_custom_call" | custom-call | flops 5368709120 | bytes 16777216 | tf_op jit(solution)/shard_map/layer/pallas_call | solution.py:434
  53.1 32.9 %hand_over.1 = bf16[128,4096]{1,0:T(8,128)(2,1)} custom-call(bf16[128,4096]{1,0:T(8,128)(2,1)} %layer.1.from_ref), custom_call_target="tpu_custom_call" | custom-call | tf_op jit(solution)/shard_map/hand_over/pallas_call | solution.py:452

commit v5 on v4

--- a/solution.py
+++ b/solution.py
@@ -262,27 +262,22 @@
 
     lax.fori_loop(0, 3 * twos, turn, 0)
 
-    span = 2 * rows
-
-    def project_rows(first):
-        here = pl.ds(pl.multiple_of(first, span), span)
-        c_rows = c_ref[here, :]
-
-        squares = jnp.zeros((span, LANES), jnp.float32)
-        for p in range(pairs):
-            inter = jnp.dot(c_rows, sr_ref[p], preferred_element_type=jnp.float32)
-            gated = yg_ref[p, here] + eg_ref[p, here] * inter
-            gated_ref[p] = gated
-            squares = squares + gated * gated
-        scale = lax.rsqrt(jnp.sum(squares, axis=1, keepdims=True) / channels + 1e-05)
-        for p in range(pairs):
-            normed_ref[:, p * LANES : (p + 1) * LANES] = (
-                gated_ref[p] * scale * gains_ref[p][0:1]
-            ).astype(jnp.bfloat16)
+    squares = jnp.zeros((length, LANES), jnp.float32)
+    for p in range(pairs):
+        inter = jnp.dot(c_ref[...], sr_ref[p], preferred_element_type=jnp.float32)
+        gated = yg_ref[p] + eg_ref[p] * inter
+        gated_ref[p] = gated
+        squares = squares + gated * gated
+    scale = lax.rsqrt(jnp.sum(squares, axis=1, keepdims=True) / channels + 1e-05)
+    for p in range(pairs):
+        normed_ref[:, p * LANES : (p + 1) * LANES] = (
+            gated_ref[p] * scale * gains_ref[p][0:1]
+        ).astype(jnp.bfloat16)
 
     def core_copy(slot, k):
+        rows_of = (y + slot) % n_y
         return remote(
-            part_ref.at[slot, k, 1 - core], core_ref.at[slot, k],
+            part_ref.at[rows_of, k, 1 - core], core_ref.at[rows_of, k],
             core_send.at[slot, k], core_recv.at[slot, k], {"tp": other_core},
         )
 
@@ -293,40 +288,36 @@
             y_send.at[slot - 1, k], y_recv.at[slot - 1, k], {"tp": target},
         )
 
-    def project(slot, k):
+    def chip_sum(slot, k):
+        core_copy(slot, k).wait_recv()
+        rows_of = (y + slot) % n_y
+        return part_ref[rows_of, k, core].astype(jnp.float32) + core_ref[rows_of, k].astype(jnp.float32)
+
+    def forward(k):
+        for slot in range(1, n_y):
+            ysend_ref[slot - 1, k] = chip_sum(slot, k).astype(jnp.bfloat16)
+            y_copy(slot, k).start()
+
+    def column(k, _):
         cols = pl.ds(pl.multiple_of(k * chunk, chunk), chunk)
         part = jnp.dot(normed_ref[...], w_ref[:, cols], preferred_element_type=jnp.float32)
         part = part.astype(jnp.bfloat16)
-        part_ref[slot, k, 0] = part[:rows]
-        part_ref[slot, k, 1] = part[rows:]
-        core_copy(slot, k).start()
-
-    def chip_sum(slot, k):
-        core_copy(slot, k).wait_recv()
-        return part_ref[slot, k, core].astype(jnp.float32) + core_ref[slot, k].astype(jnp.float32)
-
-    for slot in list(range(1, n_y)) + [0]:
-        project_rows(((y + slot) % n_y) * span)
-        if slot == (1 if n_y > 1 else 0):
-            w_copy.wait()
-
-        def forward(k, slot=slot):
-            ysend_ref[slot - 1, k] = chip_sum(slot, k).astype(jnp.bfloat16)
-            y_copy(slot, k).start()
-
-        def column(k, _, slot=slot):
-            project(slot, k)
-            if slot > 0:
-
-                @pl.when(k > 0)
-                def _():
-                    forward(k - 1)
-
-            return 0
-
-        lax.fori_loop(0, n_chunks, column, 0)
-        if slot > 0:
-            forward(n_chunks - 1)
+        for row_y in range(n_y):
+            for row_core in range(2):
+                first = (2 * row_y + row_core) * rows
+                part_ref[row_y, k, row_core] = part[first : first + rows]
+        for slot in list(range(1, n_y)) + [0]:
+            core_copy(slot, k).start()
+
+        @pl.when(k > 0)
+        def _():
+            forward(k - 1)
+
+        return 0
+
+    w_copy.wait()
+    lax.fori_loop(0, n_chunks, column, 0)
+    forward(n_chunks - 1)
 
     def out_copy(k):
         cols = pl.ds(pl.multiple_of(k * chunk, chunk), chunk)
@@ -378,7 +369,7 @@
     model = out_weight.shape[1]
     rows = length // n_tp
     n_y = n_tp // 2
-    chunk = 512
+    chunk = 256
     n_chunks = model // chunk
     state = state_maps.shape[1] // 2
     bf16, f32 = jnp.bfloat16, jnp.float32
@@ -419,8 +410,8 @@
         pltpu.VMEM((pairs, state, LANES), bf16),
         pltpu.VMEM((pairs, length, LANES), f32),
         pltpu.VMEM((pairs, length, LANES), f32),
-        pltpu.VMEM((pairs, 2 * rows, LANES), f32),
-        pltpu.VMEM((2 * rows, channels), bf16),
+        pltpu.VMEM((pairs, length, LANES), f32),
+        pltpu.VMEM((length, channels), bf16),
         pltpu.VMEM((n_y, n_chunks, 2, rows, chunk), bf16),
         pltpu.VMEM((n_y, n_chunks, rows, chunk), bf16),
         pltpu.VMEM((n_y - 1, n_chunks, rows, chunk), bf16),
@@ -431,7 +422,7 @@
         dma((n_y, n_chunks)), dma((n_y, n_chunks)),
         dma((n_y - 1, n_chunks)), dma((n_y - 1, n_chunks)),
     ]
-    mixed = pl.pallas_call(
+    return pl.pallas_call(
         functools.partial(layer_kernel, n_ctx, n_tp, chunk),
         out_shape=jax.ShapeDtypeStruct((rows, model), bf16),
         in_specs=[anywhere] * 3 + [vmem] * 7 + [anywhere],
@@ -449,26 +440,6 @@
         x_inputs, state_maps, z_gate, step_raw.T, step_bias[None], decay_log[None], skip_gain[None],
         x_filter, state_filter, norm_gain[None], out_weight,
     )
-    return pl.pallas_call(
-        hand_over,
-        out_shape=jax.ShapeDtypeStruct((rows, model), bf16),
-        in_specs=[anywhere],
-        out_specs=anywhere,
-        scratch_shapes=[dma((4,))],
-        name="hand_over",
-    )(mixed)
-
-
-def hand_over(from_ref, to_ref, sems):
-    part = from_ref.shape[0] // 4
-    copies = [
-        pltpu.make_async_copy(from_ref.at[pl.ds(i * part, part)], to_ref.at[pl.ds(i * part, part)], sems.at[i])
-        for i in range(4)
-    ]
-    for copy in copies:
-        copy.start()
-    for copy in copies:
-        copy.wait()
 
 
 def solution(mesh):

time: 86.6 us -> 56.8 us (0.66)
  Pallas kernels: 86 us -> 53.9 us
  local copies, waits for them, and re-layouts: 0 us -> 2.29 us
    pallas_call x1 -> x0, Pallas kernels: 32.9 us -> none  [on_device(): pl.pallas_call(hand_over, out_shape=jax.ShapeDtypeStruct((rows, model), b...]
    unnamed x0 -> x1, local copies, waits for them, and re-layouts: none -> 2.29 us
where the time goes in v5:
time: 56.8 us; the launch traced here: 56.2 us
  Pallas kernels  53.9 us (95%)
  local copies, waits for them, and re-layouts  2.29 us (4%)
    pallas_call x1, Pallas kernels, on_device(): pl.pallas_call(functools.partial(layer_kernel, n_ctx, n_tp, chunk), out_s...  53.9 us
    unnamed x1, local copies, waits for them, and re-layouts  2.29 us

profile of v5, /device:TPU:25, one launch (start us, length us, event | category | flops | bytes accessed | tf_op | source)
XLA Modules:
  0.0 56.2 jit_solution(14828648945687621456)
XLA Ops:
  0.0 53.9 %layer.1 = bf16[128,4096]{1,0:T(8,128)(2,1)} custom-call(bf16[512,1024]{1,0:T(8,128)(2,1)} %x_hbm.1, bf16[512,256]{1,0:T(8,128)(2,1)} %m_hbm.1, bf16[512,1024]{1,0:T(8,128)(2,1)} %z_hbm.1, f32[16,512]{1,0:T(8,128)} %bitcast.5, f32[1,16]{1,0:T(1,128)} %bitcast.7, f32[1,16]{1,0:T(1,128)} %bitcast.8, f32[1,16]{1,0:T(1,128)} %bitcast.9, bf16[4,1024]{1,0:T(4,128)(2,1)} %xf_ref.1, ...), custom_call_target="tpu_custom_call" | custom-call | flops 5368709120 | bytes 16777216 | tf_op jit(solution)/shard_map/layer/pallas_call | solution.py:425
  54.0 2.3 %copy.13 = bf16[128,4096]{1,0:T(8,128)(2,1)} copy(bf16[128,4096]{1,0:T(8,128)(2,1)} %layer.1) | data formatting | bytes 2097152

commit v6 on v5

--- a/solution.py
+++ b/solution.py
@@ -23,7 +23,7 @@
     out_ref,
     w_ref, x_ref, m_ref, z_ref, hx_ref, hm_ref, pad_ref, xfs_ref, mfs_ref, gains_ref, skips_ref,
     sq_ref, parts_ref, left_ref, pick_ref, dsend_ref, drecv_ref,
-    xc_ref, uc_ref, aexp_ref, mid_ref, first_ref, bt_ref, c_ref, cb_ref, lown_ref, lsend_ref, lrecv_ref, csend_ref, crecv_ref, sr_ref,
+    xc_ref, uc_ref, mid_ref, first_ref, bt_ref, c_ref, cb_ref, lown_ref, lsend_ref, lrecv_ref, csend_ref, crecv_ref, sr_ref,
     yg_ref, eg_ref, gated_ref, normed_ref, part_ref, core_ref, ysend_ref, yrecv_ref, out_buf,
     w_sem, in_sem, out_sem, halo_send, halo_recv, dec_send, dec_recv, pair_send, pair_recv, chain_send, chain_recv,
     core_send, core_recv, y_send, y_recv,
@@ -48,8 +48,13 @@
     z_copy = pltpu.make_async_copy(z_hbm, z_ref, in_sem.at[2])
 
     barrier = pltpu.get_barrier_semaphore()
-    for off in (1, n_ctx - 1, 2, n_ctx - 2):
-        pl.semaphore_signal(barrier, inc=1, device_id={"ctx": (ctx + off) % n_ctx}, device_id_type=MESH)
+    has_prev, has_next = ctx >= 1, ctx <= n_ctx - 2
+    for there, off in ((has_prev, -1), (has_next, 1), (ctx >= 2, -2), (ctx <= n_ctx - 3, 2)):
+
+        @pl.when(there)
+        def _(off=off):
+            pl.semaphore_signal(barrier, inc=1, device_id={"ctx": ctx + off}, device_id_type=MESH)
+
     pl.semaphore_signal(barrier, inc=1, device_id={"tp": other_core}, device_id_type=MESH)
     for off in range(1, n_y):
         pl.semaphore_signal(
@@ -81,13 +86,23 @@
     rate = step * jnp.exp(all_tokens(lane_column(decay_ref)))
     skip_t = lane_column(skip_ref)
 
-    pl.semaphore_wait(barrier, 4 + 1 + (n_y - 1))
+    greeted = jnp.minimum(ctx, 2) + jnp.minimum(n_ctx - 1 - ctx, 2)
+    pl.semaphore_wait(barrier, greeted + 1 + (n_y - 1))
 
     following = {"ctx": (ctx + 1) % n_ctx}
     halo_x = remote(x_hbm.at[pl.ds(length - HALO, HALO)], hx_ref, halo_send.at[0], halo_recv.at[0], following)
     halo_m = remote(m_hbm.at[pl.ds(length - HALO, HALO)], hm_ref, halo_send.at[1], halo_recv.at[1], following)
-    halo_m.start()
-    halo_x.start()
+
+    @pl.when(has_next)
+    def _():
+        halo_m.start()
+        halo_x.start()
+
+    @pl.when(ctx == 0)
+    def _():
+        hm_ref[...] = jnp.zeros_like(hm_ref)
+        hx_ref[...] = jnp.zeros_like(hx_ref)
+
 
     s_ids = lax.broadcasted_iota(jnp.int32, (length, length), 0)
     t_ids = lax.broadcasted_iota(jnp.int32, (length, length), 1)
@@ -121,20 +136,24 @@
     match = (lane >= (term & (heads - 1)) * width) & (lane < ((term & (heads - 1)) + 1) * width)
     pick_sum = jnp.where(match & (term < 3 * heads), 1.0, 0.0).astype(jnp.bfloat16)
     pick_source = jnp.where(match & (term >= 3 * heads) & (term < 6 * heads), 1.0, 0.0).astype(jnp.bfloat16)
-    last = jnp.dot(left_ref[length - HALO :, :], pick_sum, preferred_element_type=jnp.float32)[HALO - 1 :]
+    quarter = length // 4
+    few = jnp.concatenate([left_ref[(j + 1) * quarter - HALO : (j + 1) * quarter, :] for j in range(4)], axis=0)
+    few = jnp.dot(few, pick_sum, preferred_element_type=jnp.float32)
     for p in range(pairs):
         cols = slice(p * LANES, (p + 1) * LANES)
         pick_ref[p, :, :LANES] = pick_sum[:, cols]
         pick_ref[p, :, LANES:] = pick_source[:, cols]
-        dsend_ref[p] = jnp.broadcast_to(last[:, cols], (8, LANES))
+        for j in range(4):
+            row = few[(j + 1) * HALO - 1 : (j + 1) * HALO, cols]
+            mid_ref[p, j] = jnp.broadcast_to(row, (8, LANES))
+        dsend_ref[p] = jnp.broadcast_to(few[4 * HALO - 1 :, cols], (8, LANES))
     dec_copy = remote(dsend_ref, drecv_ref, dec_send, dec_recv, {"ctx": mate})
     dec_copy.start()
 
     taps = xf_ref.shape[0]
-    has_prev = jnp.where(ctx > 0, 1.0, 0.0).astype(jnp.float32)
 
     def conv(block, halo, filters, slot):
-        pad_ref[slot, 0:8] = halo.astype(jnp.float32)[HALO - 8 :] * has_prev
+        pad_ref[slot, 0:8] = halo.astype(jnp.float32)[HALO - 8 :]
         pad_ref[slot, 8:] = block.astype(jnp.float32)
         total = filters[0:1] * pad_ref[slot, 9 - taps : 9 - taps + length]
         for k in range(1, taps):
@@ -143,11 +162,14 @@
         return half_silu(total)
 
     m_copy.wait()
-    halo_m.wait_recv()
+
+    @pl.when(has_prev)
+    def _():
+        halo_m.wait_recv()
+        halo_x.wait_recv()
+
     bt_ref[...] = conv(m_ref[:, :LANES], hm_ref[:, :LANES], mfs_ref[0], 0).T.astype(jnp.bfloat16)
-    c_ref[...] = conv(m_ref[:, LANES:], hm_ref[:, LANES:], mfs_ref[1], 1).astype(jnp.bfloat16)
     x_copy.wait()
-    halo_x.wait_recv()
 
     def pair_copy(p):
         return remote(lsend_ref.at[p], lrecv_ref.at[p], pair_send.at[p], pair_recv.at[p], {"ctx": mate})
@@ -158,17 +180,14 @@
         cols = pl.ds(pl.multiple_of(p * LANES, LANES), LANES)
         xc = conv(x_ref[:, cols], hx_ref[:, cols], xfs_ref[p], slot).astype(jnp.bfloat16)
         xc_ref[p] = xc
-        both = jnp.dot(left_ref[...], pick_ref[p], preferred_element_type=jnp.float32)
-        sums, source = both[:, :LANES], both[:, LANES:]
-        aexp_ref[p] = sums
+        source = jnp.dot(left_ref[...], pick_ref[p, :, LANES:], preferred_element_type=jnp.float32)
         wide = xc.astype(jnp.float32)
         end = dsend_ref[p][0:1]
-        border = sums[half - 1 : half]
+        border = mid_ref[p, 1][0:1]
         mids, states = [], []
         for j, stop in ((0, border), (1, end)):
             here = slice(j * half, (j + 1) * half)
-            mid = sums[j * half + half // 2 - 1 : j * half + half // 2]
-            mid_ref[p, j] = jnp.broadcast_to(mid, (8, LANES))
+            mid = mid_ref[p, 2 * j][0:1]
             u = (jnp.exp(source[here] - mid) * wide[here]).astype(jnp.bfloat16)
             uc_ref[p, here] = u
             fresh = jnp.dot(bt_ref[:, here], u, preferred_element_type=jnp.float32)
@@ -180,13 +199,6 @@
         lsend_ref[p] = state.astype(jnp.bfloat16)
         pair_copy(p).start()
 
-    row_half = lax.broadcasted_iota(jnp.int32, (half, half), 0)
-    col_half = lax.broadcasted_iota(jnp.int32, (half, half), 1)
-    for j in range(2):
-        here = slice(j * half, (j + 1) * half)
-        scores = jnp.dot(c_ref[here, :], bt_ref[:, here], preferred_element_type=jnp.float32)
-        cb_ref[j] = jnp.where(row_half >= col_half, scores, 0.0).astype(jnp.bfloat16)
-
     is_odd = odd.astype(jnp.float32)
     is_even = 1.0 - is_odd
     next_pair = {"ctx": (ctx + 2) % n_ctx}
@@ -224,16 +236,26 @@
             csend_ref[p] = (d_odd * middle + l_odd).astype(jnp.bfloat16)
             chain_copy(p).start()
 
+    def scores_of_halves():
+        c_ref[...] = conv(m_ref[:, LANES:], hm_ref[:, LANES:], mfs_ref[1], 1).astype(jnp.bfloat16)
+        row_half = lax.broadcasted_iota(jnp.int32, (half, half), 0)
+        col_half = lax.broadcasted_iota(jnp.int32, (half, half), 1)
+        for j in range(2):
+            here = slice(j * half, (j + 1) * half)
+            scores = jnp.dot(c_ref[here, :], bt_ref[:, here], preferred_element_type=jnp.float32)
+            cb_ref[j] = jnp.where(row_half >= col_half, scores, 0.0).astype(jnp.bfloat16)
+
     def within(p):
         cols = pl.ds(pl.multiple_of(p * LANES, LANES), LANES)
         skip = skips_ref[p][0:1]
+        sums = jnp.dot(left_ref[...], pick_ref[p, :, :LANES], preferred_element_type=jnp.float32)
         for j in range(2):
             here = slice(j * half, (j + 1) * half)
             own = jnp.dot(cb_ref[j], uc_ref[p, here], preferred_element_type=jnp.float32)
             if j == 1:
                 own = own + jnp.dot(c_ref[here, :], first_ref[p], preferred_element_type=jnp.float32)
-            mid = mid_ref[p, j][0:1]
-            decay = jnp.exp(mid - aexp_ref[p, here])
+            mid = mid_ref[p, 2 * j][0:1]
+            decay = jnp.exp(mid - sums[here])
             gate = half_silu(z_ref[here, cols].astype(jnp.float32))
             yg_ref[p, here] = (decay * own + skip * xc_ref[p, here].astype(jnp.float32)) * gate
             eg_ref[p, here] = decay * jnp.exp(-mid) * gate
@@ -252,6 +274,10 @@
         def _():
             for slot in range(2):
                 local_state(2 * i + slot, slot)
+
+        @pl.when(i == twos)
+        def _():
+            scores_of_halves()
 
         @pl.when((i >= twos) & (i < 2 * twos))
         def _():
@@ -334,8 +360,11 @@
 
     lax.fori_loop(0, n_chunks, finish, 0)
 
-    halo_m.wait_send()
-    halo_x.wait_send()
+    @pl.when(has_next)
+    def _():
+        halo_m.wait_send()
+        halo_x.wait_send()
+
     dec_copy.wait_send()
 
     def drain_states(p, _):
@@ -396,8 +425,7 @@
         pltpu.VMEM((pairs, 8, LANES), f32),
         pltpu.VMEM((pairs, length, LANES), bf16),
         pltpu.VMEM((pairs, length, LANES), bf16),
-        pltpu.VMEM((pairs, length, LANES), f32),
-        pltpu.VMEM((pairs, 2, 8, LANES), f32),
+        pltpu.VMEM((pairs, 4, 8, LANES), f32),
         pltpu.VMEM((pairs, state, LANES), bf16),
         pltpu.VMEM((state, length), bf16),
         pltpu.VMEM((length, state), bf16),

time: 56.8 us -> 54.5 us (0.960)
  Pallas kernels: 53.9 us -> 52 us
    pallas_call x1, Pallas kernels: 53.9 us -> 52 us  [on_device(): pl.pallas_call(functools.partial(layer_kernel, n_ctx, n_tp, chunk), out_s...]
where the time goes in v6:
time: 54.5 us; the launch traced here: 54.3 us
  Pallas kernels  52 us (95%)
  local copies, waits for them, and re-layouts  2.29 us (4%)
    pallas_call x1, Pallas kernels, on_device(): pl.pallas_call(functools.partial(layer_kernel, n_ctx, n_tp, chunk), out_s...  52 us
    unnamed x1, local copies, waits for them, and re-layouts  2.29 us

profile of v6, /device:TPU:25, one launch (start us, length us, event | category | flops | bytes accessed | tf_op | source)
XLA Modules:
  0.0 54.3 jit_solution(17385835696896661222)
XLA Ops:
  0.0 52.0 %layer.1 = bf16[128,4096]{1,0:T(8,128)(2,1)} custom-call(bf16[512,1024]{1,0:T(8,128)(2,1)} %x_hbm.1, bf16[512,256]{1,0:T(8,128)(2,1)} %m_hbm.1, bf16[512,1024]{1,0:T(8,128)(2,1)} %z_hbm.1, f32[16,512]{1,0:T(8,128)} %bitcast.5, f32[1,16]{1,0:T(1,128)} %bitcast.7, f32[1,16]{1,0:T(1,128)} %bitcast.8, f32[1,16]{1,0:T(1,128)} %bitcast.9, bf16[4,1024]{1,0:T(4,128)(2,1)} %xf_ref.1, ...), custom_call_target="tpu_custom_call" | custom-call | flops 5368709120 | bytes 16777216 | tf_op jit(solution)/shard_map/layer/pallas_call | solution.py:453
  52.0 2.3 %copy.13 = bf16[128,4096]{1,0:T(8,128)(2,1)} copy(bf16[128,4096]{1,0:T(8,128)(2,1)} %layer.1) | data formatting | bytes 2097152

commit v7 on v6

--- a/solution.py
+++ b/solution.py
@@ -22,9 +22,9 @@
     x_hbm, m_hbm, z_hbm, step_ref, bias_ref, decay_ref, skip_ref, xf_ref, mf_ref, gain_ref, w_hbm,
     out_ref,
     w_ref, x_ref, m_ref, z_ref, hx_ref, hm_ref, pad_ref, xfs_ref, mfs_ref, gains_ref, skips_ref,
-    sq_ref, parts_ref, left_ref, pick_ref, dsend_ref, drecv_ref,
+    parts_ref, left_ref, pick_ref, dsend_ref, drecv_ref,
     xc_ref, uc_ref, mid_ref, first_ref, bt_ref, c_ref, cb_ref, lown_ref, lsend_ref, lrecv_ref, csend_ref, crecv_ref, sr_ref,
-    yg_ref, eg_ref, gated_ref, normed_ref, part_ref, core_ref, ysend_ref, yrecv_ref, out_buf,
+    yg_ref, eg_ref, squares_ref, gated_ref, normed_ref, part_ref, core_ref, ysend_ref, yrecv_ref, out_buf,
     w_sem, in_sem, out_sem, halo_send, halo_recv, dec_send, dec_recv, pair_send, pair_recv, chain_send, chain_recv,
     core_send, core_recv, y_send, y_recv,
 ):
@@ -69,22 +69,20 @@
             src_ref=src, dst_ref=dst, send_sem=send, recv_sem=recv, device_id=where, device_id_type=MESH
         )
 
-    def lane_column(ref):
-        sq_ref[...] = jnp.zeros_like(sq_ref)
-        sq_ref[:, :heads] = jnp.broadcast_to(ref[...], (LANES, heads))
-        return sq_ref[...].T
-
     def three_terms(v):
         first = v.astype(jnp.bfloat16).astype(jnp.float32)
         second = (v - first).astype(jnp.bfloat16).astype(jnp.float32)
         return [first, second, (v - first - second).astype(jnp.bfloat16).astype(jnp.float32)]
 
     def all_tokens(column):
-        return jnp.concatenate([column[:heads]] * (length // LANES), axis=1)
-
-    step = jnp.log(1.0 + jnp.exp(step_ref[...] + all_tokens(lane_column(bias_ref))))
-    rate = step * jnp.exp(all_tokens(lane_column(decay_ref)))
-    skip_t = lane_column(skip_ref)
+        return jnp.concatenate([column] * (length // LANES), axis=1)
+
+    filling = jnp.zeros((1, LANES - 3 * heads), jnp.float32)
+    vectors = jnp.concatenate([bias_ref[...], decay_ref[...], skip_ref[...], filling], axis=1)
+    columns = jnp.broadcast_to(vectors, (LANES, LANES)).T
+    step = jnp.log(1.0 + jnp.exp(step_ref[...] + all_tokens(columns[:heads])))
+    rate = step * jnp.exp(all_tokens(columns[heads : 2 * heads]))
+    skip_t = columns[2 * heads : 3 * heads]
 
     greeted = jnp.minimum(ctx, 2) + jnp.minimum(n_ctx - 1 - ctx, 2)
     pl.semaphore_wait(barrier, greeted + 1 + (n_y - 1))
@@ -264,37 +262,45 @@
     twos = pairs // 2
     lag = jnp.minimum(2 + 2 * z, 2 * twos)
 
-    def turn(i, _):
-        @pl.when((i >= lag) & (i < lag + twos))
-        def _():
-            for slot in range(2):
-                relay(2 * (i - lag) + slot)
-
-        @pl.when(i < twos)
-        def _():
-            for slot in range(2):
-                local_state(2 * i + slot, slot)
-
-        @pl.when(i == twos)
-        def _():
-            scores_of_halves()
-
-        @pl.when((i >= twos) & (i < 2 * twos))
-        def _():
-            for slot in range(2):
-                within(2 * (i - twos) + slot)
-
-        return 0
-
-    lax.fori_loop(0, 3 * twos, turn, 0)
-
-    squares = jnp.zeros((length, LANES), jnp.float32)
-    for p in range(pairs):
+    gate_lag = jnp.maximum(lag, twos)
+    squares_ref[...] = jnp.zeros_like(squares_ref)
+
+    def gate_rows(p):
         inter = jnp.dot(c_ref[...], sr_ref[p], preferred_element_type=jnp.float32)
         gated = yg_ref[p] + eg_ref[p] * inter
         gated_ref[p] = gated
-        squares = squares + gated * gated
-    scale = lax.rsqrt(jnp.sum(squares, axis=1, keepdims=True) / channels + 1e-05)
+        squares_ref[...] += gated * gated
+
+    def turn(i, _):
+        @pl.when(i < twos)
+        def _():
+            for slot in range(2):
+                local_state(2 * i + slot, slot)
+
+        @pl.when((i >= lag) & (i < lag + twos))
+        def _():
+            for slot in range(2):
+                relay(2 * (i - lag) + slot)
+
+        @pl.when(i == twos)
+        def _():
+            scores_of_halves()
+
+        @pl.when((i >= twos) & (i < 2 * twos))
+        def _():
+            for slot in range(2):
+                within(2 * (i - twos) + slot)
+
+        @pl.when((i >= gate_lag) & (i < gate_lag + twos))
+        def _():
+            for slot in range(2):
+                gate_rows(2 * (i - gate_lag) + slot)
+
+        return 0
+
+    lax.fori_loop(0, 3 * twos, turn, 0)
+
+    scale = lax.rsqrt(jnp.sum(squares_ref[...], axis=1, keepdims=True) / channels + 1e-05)
     for p in range(pairs):
         normed_ref[:, p * LANES : (p + 1) * LANES] = (
             gated_ref[p] * scale * gains_ref[p][0:1]
@@ -417,7 +423,6 @@
         pltpu.VMEM((2, x_filter.shape[0], LANES), f32),
         pltpu.VMEM((pairs, 8, LANES), f32),
         pltpu.VMEM((pairs, 8, LANES), f32),
-        pltpu.VMEM((LANES, LANES), f32),
         pltpu.VMEM((LANES, length), f32),
         pltpu.VMEM((length, LANES), bf16),
         pltpu.VMEM((pairs, LANES, 2 * LANES), bf16),
@@ -438,6 +443,7 @@
         pltpu.VMEM((pairs, state, LANES), bf16),
         pltpu.VMEM((pairs, length, LANES), f32),
         pltpu.VMEM((pairs, length, LANES), f32),
+        pltpu.VMEM((length, LANES), f32),
         pltpu.VMEM((pairs, length, LANES), f32),
         pltpu.VMEM((length, channels), bf16),
         pltpu.VMEM((n_y, n_chunks, 2, rows, chunk), bf16),

time: 54.5 us -> 53.4 us (0.980)
  Pallas kernels: 52 us -> 50.9 us
    pallas_call x1, Pallas kernels: 52 us -> 50.9 us  [on_device(): pl.pallas_call(functools.partial(layer_kernel, n_ctx, n_tp, chunk), out_s...]
where the time goes in v7:
time: 53.4 us; the launch traced here: 53.2 us
  Pallas kernels  50.9 us (95%)
  local copies, waits for them, and re-layouts  2.29 us (4%)
    pallas_call x1, Pallas kernels, on_device(): pl.pallas_call(functools.partial(layer_kernel, n_ctx, n_tp, chunk), out_s...  50.9 us
    unnamed x1, local copies, waits for them, and re-layouts  2.29 us

profile of v7, /device:TPU:25, one launch (start us, length us, event | category | flops | bytes accessed | tf_op | source)
XLA Modules:
  0.0 53.2 jit_solution(4938759102628946649)
XLA Ops:
  0.0 50.9 %layer.1 = bf16[128,4096]{1,0:T(8,128)(2,1)} custom-call(bf16[512,1024]{1,0:T(8,128)(2,1)} %x_hbm.1, bf16[512,256]{1,0:T(8,128)(2,1)} %m_hbm.1, bf16[512,1024]{1,0:T(8,128)(2,1)} %z_hbm.1, f32[16,512]{1,0:T(8,128)} %bitcast.5, f32[1,16]{1,0:T(1,128)} %bitcast.7, f32[1,16]{1,0:T(1,128)} %bitcast.8, f32[1,16]{1,0:T(1,128)} %bitcast.9, bf16[4,1024]{1,0:T(4,128)(2,1)} %xf_ref.1, ...), custom_call_target="tpu_custom_call" | custom-call | flops 5368709120 | bytes 16777216 | tf_op jit(solution)/shard_map/layer/pallas_call | solution.py:459
  50.9 2.3 %copy.13 = bf16[128,4096]{1,0:T(8,128)(2,1)} copy(bf16[128,4096]{1,0:T(8,128)(2,1)} %layer.1) | data formatting | bytes 2097152

commit v8 on v7

--- a/solution.py
+++ b/solution.py
@@ -338,7 +338,7 @@
             for row_core in range(2):
                 first = (2 * row_y + row_core) * rows
                 part_ref[row_y, k, row_core] = part[first : first + rows]
-        for slot in list(range(1, n_y)) + [0]:
+        for slot in range(1, n_y):
             core_copy(slot, k).start()
 
         @pl.when(k > 0)
@@ -350,6 +350,12 @@
     w_copy.wait()
     lax.fori_loop(0, n_chunks, column, 0)
     forward(n_chunks - 1)
+
+    def share_own(k, _):
+        core_copy(0, k).start()
+        return 0
+
+    lax.fori_loop(0, n_chunks, share_own, 0)
 
     def out_copy(k):
         cols = pl.ds(pl.multiple_of(k * chunk, chunk), chunk)

time: 53.4 us -> 53.4 us (level)
  no operation moved by 1% of the time
where the time goes in v8:
time: 53.4 us; the launch traced here: 53.1 us
  Pallas kernels  50.8 us (95%)
  local copies, waits for them, and re-layouts  2.29 us (4%)
    pallas_call x1, Pallas kernels, on_device(): pl.pallas_call(functools.partial(layer_kernel, n_ctx, n_tp, chunk), out_s...  50.8 us
    unnamed x1, local copies, waits for them, and re-layouts  2.29 us

profile of v8, /device:TPU:25, one launch (start us, length us, event | category | flops | bytes accessed | tf_op | source)
XLA Modules:
  0.0 53.1 jit_solution(14240947589382678256)
XLA Ops:
  0.0 50.8 %layer.1 = bf16[128,4096]{1,0:T(8,128)(2,1)} custom-call(bf16[512,1024]{1,0:T(8,128)(2,1)} %x_hbm.1, bf16[512,256]{1,0:T(8,128)(2,1)} %m_hbm.1, bf16[512,1024]{1,0:T(8,128)(2,1)} %z_hbm.1, f32[16,512]{1,0:T(8,128)} %bitcast.5, f32[1,16]{1,0:T(1,128)} %bitcast.7, f32[1,16]{1,0:T(1,128)} %bitcast.8, f32[1,16]{1,0:T(1,128)} %bitcast.9, bf16[4,1024]{1,0:T(4,128)(2,1)} %xf_ref.1, ...), custom_call_target="tpu_custom_call" | custom-call | flops 5368709120 | bytes 16777216 | tf_op jit(solution)/shard_map/layer/pallas_call | solution.py:465
  50.9 2.3 %copy.13 = bf16[128,4096]{1,0:T(8,128)(2,1)} copy(bf16[128,4096]{1,0:T(8,128)(2,1)} %layer.1) | data formatting | bytes 2097152

commit v9 on v8

--- a/solution.py
+++ b/solution.py
@@ -410,7 +410,7 @@
     model = out_weight.shape[1]
     rows = length // n_tp
     n_y = n_tp // 2
-    chunk = 256
+    chunk = 512
     n_chunks = model // chunk
     state = state_maps.shape[1] // 2
     bf16, f32 = jnp.bfloat16, jnp.float32

time: 53.4 us -> 53.4 us (level)
  no operation moved by 1% of the time
where the time goes in v9:
time: 53.4 us; the launch traced here: 53.2 us
  Pallas kernels  50.9 us (95%)
  local copies, waits for them, and re-layouts  2.29 us (4%)
    pallas_call x1, Pallas kernels, on_device(): pl.pallas_call(functools.partial(layer_kernel, n_ctx, n_tp, chunk), out_s...  50.9 us
    unnamed x1, local copies, waits for them, and re-layouts  2.29 us

profile of v9, /device:TPU:25, one launch (start us, length us, event | category | flops | bytes accessed | tf_op | source)
XLA Modules:
  0.0 53.2 jit_solution(1967069280737029102)
XLA Ops:
  0.0 50.9 %layer.1 = bf16[128,4096]{1,0:T(8,128)(2,1)} custom-call(bf16[512,1024]{1,0:T(8,128)(2,1)} %x_hbm.1, bf16[512,256]{1,0:T(8,128)(2,1)} %m_hbm.1, bf16[512,1024]{1,0:T(8,128)(2,1)} %z_hbm.1, f32[16,512]{1,0:T(8,128)} %bitcast.5, f32[1,16]{1,0:T(1,128)} %bitcast.7, f32[1,16]{1,0:T(1,128)} %bitcast.8, f32[1,16]{1,0:T(1,128)} %bitcast.9, bf16[4,1024]{1,0:T(4,128)(2,1)} %xf_ref.1, ...), custom_call_target="tpu_custom_call" | custom-call | flops 5368709120 | bytes 16777216 | tf_op jit(solution)/shard_map/layer/pallas_call | solution.py:465
  50.9 2.3 %copy.13 = bf16[128,4096]{1,0:T(8,128)(2,1)} copy(bf16[128,4096]{1,0:T(8,128)(2,1)} %layer.1) | data formatting | bytes 2097152
